TPU v7x, 256 devices: a whole 4x4x8 slice. The times are simulated.
256 devices in a mesh: leaf: 128 (over y, x, z), rhs: 2 (over core).
Axes of the slice: x: 4, y: 4, z: 8, core: 2. Of those that a mesh axis runs over, the one named last changes fastest.
Arguments:
- charges: bfloat16 [2048, 256, 256], P('leaf', None, 'rhs'), may hold values from -6 to 6
- leaf_basis: bfloat16 [2048, 256, 128], P('leaf'), may hold values from -0.375 to 0.375
- transfer3: bfloat16 [2048, 128, 128], P('leaf'), may hold values from -0.375 to 0.375
- transfer2: bfloat16 [128, 128, 128], P('leaf'), may hold values from -0.375 to 0.375
- transfer1: bfloat16 [16, 128, 128], replicated, may hold values from -0.375 to 0.375
- coupling3: bfloat16 [2048, 8, 128, 128], P('leaf'), may hold values from -0.1875 to 0.1875
- coupling2: bfloat16 [128, 4, 128, 128], P('leaf'), may hold values from -0.25 to 0.25
- coupling1: bfloat16 [16, 4, 128, 128], replicated, may hold values from -0.25 to 0.25
- coupling0: bfloat16 [4, 128, 128], replicated, may hold values from -0.5 to 0.5
- near_blocks: bfloat16 [2048, 6, 256, 256], P('leaf', 'rhs'), may hold values from -0.15625 to 0.15625
- near_list: int32 [2048, 6], P('leaf'), may hold values from 0 to 2047, as said below
- far_list3: int32 [2048, 8], P('leaf'), may hold values from 0 to 2047, as said below
- far_list2: int32 [128, 4], P('leaf'), may hold values from 0 to 127, as said below
- far_list1: int32 [16, 4], replicated, may hold values from 0 to 15, as said below
- far_list0: int32 [4], replicated, may hold values from 0 to 3, as said below
Outputs:
- potential: bfloat16 [2048, 256, 256], P('leaf', None, 'rhs')
Inputs may be any that keep to these rules, and one draw needn't show every extreme that they name: `near_list`: each named leaf lies at most 8 places from the row's leaf in leaf order; the first entry is the leaf itself. `far_list3`: each named leaf lies more than 8 and at most 16 places from the row's leaf in leaf order. `far_list2`: each named node lies one or two places from the row's node. `far_list1`: never the row's node nor a node beside it in cyclic order. `far_list0`: never the row's node.
All inputs are finite; a program needn't handle non-finite values.
Results may differ from a plain program's by a relative error of at most 0.019.
Values may be sent and summed in bfloat16 or wider, within the bound.
No kernel may reach another device: no remote copies, remote signals or barrier semaphores. Data moves between devices by JAX's collectives and lax.ppermute only.
A program may use at most 128 MiB of HBM per device.

v0:
```python
import jax
import jax.numpy as jnp
from jax import lax
from jax.sharding import PartitionSpec as P

TOP1 = 16
TOP0 = 4


def passed_along(block, axis, distance):
    devices = range(lax.axis_size(axis))
    route = [(i - distance, i) for i in devices if i - distance in devices]
    return lax.ppermute(block, axis, route)


def extended(block, sides, width):
    for axis, dim in sides:
        count = lax.axis_size(axis)
        forward = [(i, i + 1) for i in range(count - 1)]
        backward = [(target, source) for source, target in forward]
        low = lax.ppermute(
            lax.slice_in_dim(block, block.shape[dim] - width, None, axis=dim), axis, forward
        )
        high = lax.ppermute(lax.slice_in_dim(block, 0, width, axis=dim), axis, backward)
        block = jnp.concatenate([low, block, high], axis=dim)
    return block


def neighbour(values, shift_by):
    return passed_along(values, "leaf", shift_by)


def upper_levels(moments1, transfer1, coupling1, coupling0, far_list1, far_list0):
    fan_ratio = TOP1 // TOP0
    width = moments1.shape[2]
    terms0 = jnp.einsum("qkj,qkc->qjc", transfer1, moments1, preferred_element_type=jnp.float32)
    moments0 = (
        terms0.reshape(TOP0, fan_ratio, moments1.shape[1], width).sum(axis=1).astype(jnp.bfloat16)
    )
    local0 = jnp.einsum(
        "rkj,rjc->rkc",
        coupling0,
        jnp.take(moments0, far_list0, axis=0),
        preferred_element_type=jnp.float32,
    ).astype(jnp.bfloat16)
    parents0 = jnp.repeat(local0, fan_ratio, axis=0)
    local1 = jnp.einsum(
        "qfkj,qfjc->qkc",
        coupling1,
        jnp.take(moments1, far_list1, axis=0),
        preferred_element_type=jnp.float32,
    )
    local1 = local1 + jnp.einsum(
        "qkj,qjc->qkc", transfer1, parents0, preferred_element_type=jnp.float32
    )
    return local1.astype(jnp.bfloat16)


def body(
    charges,
    leaf_basis,
    transfer3,
    transfer2,
    transfer1,
    coupling3,
    coupling2,
    coupling1,
    coupling0,
    near_blocks,
    near_list,
    far_list3,
    far_list2,
    far_list1,
    far_list0,
):
    leaf_count = charges.shape[0]
    half_width = leaf_count // 2
    device = lax.axis_index("leaf")
    first_leaf = device * leaf_count
    moments3 = jnp.einsum(
        "gbk,gbc->gkc", leaf_basis, charges, preferred_element_type=jnp.float32
    ).astype(jnp.bfloat16)
    moments2 = jnp.einsum(
        "gkj,gkc->jc", transfer3, moments3, preferred_element_type=jnp.float32
    ).astype(jnp.bfloat16)
    term_one = jnp.einsum("kj,kc->jc", transfer2[0], moments2, preferred_element_type=jnp.float32)
    widened = extended(charges, (("leaf", 0),), half_width)
    near_index = near_list - first_leaf + half_width
    sources = jnp.take(widened, near_index, axis=0)
    near_part = jnp.einsum(
        "gsab,gsbc->gac",
        lax.all_gather(near_blocks, "rhs", axis=1, tiled=True),
        sources,
        preferred_element_type=jnp.float32,
    )
    beside_all = extended(moments3, (("leaf", 0),), leaf_count)
    sources3 = jnp.take(beside_all, far_list3 - first_leaf + leaf_count, axis=0)
    far_part3 = jnp.einsum(
        "gfkj,gfjc->gkc", coupling3, sources3, preferred_element_type=jnp.float32
    )
    offsets = (-2, -1, 1, 2)
    nearby = jnp.stack([neighbour(moments2, -offset_value) for offset_value in offsets])
    wanted = far_list2[0] - device
    select = (wanted[:, None] == jnp.array(offsets, jnp.int32)[None, :]).astype(jnp.bfloat16)
    chosen = jnp.einsum("fo,okc->fkc", select, nearby, preferred_element_type=jnp.float32).astype(
        jnp.bfloat16
    )
    far_part2 = jnp.einsum("fkj,fjc->kc", coupling2[0], chosen, preferred_element_type=jnp.float32)
    group_size = lax.axis_size("leaf") // TOP1
    owner_node = device // group_size
    placed = (jnp.arange(TOP1) == owner_node).astype(jnp.float32)[:, None, None] * term_one[None]
    moments1 = lax.psum(placed, "leaf").astype(jnp.bfloat16)
    local1 = upper_levels(moments1, transfer1, coupling1, coupling0, far_list1, far_list0)
    parent = lax.dynamic_index_in_dim(local1, owner_node, 0, keepdims=False)
    local2 = (
        far_part2
        + jnp.einsum("kj,jc->kc", transfer2[0], parent, preferred_element_type=jnp.float32)
    ).astype(jnp.bfloat16)
    local3 = (
        far_part3 + jnp.einsum("gkj,jc->gkc", transfer3, local2, preferred_element_type=jnp.float32)
    ).astype(jnp.bfloat16)
    potential = (
        jnp.einsum("gbk,gkc->gbc", leaf_basis, local3, preferred_element_type=jnp.float32)
        + near_part
    )
    return potential.astype(jnp.bfloat16)


def solution(mesh):
    placed = (
        P("leaf", None, "rhs"),
        P("leaf", None, None),
        P("leaf", None, None),
        P("leaf", None, None),
        P(),
        P("leaf", None, None, None),
        P("leaf", None, None, None),
        P(),
        P(),
        P("leaf", "rhs", None, None),
        P("leaf", None),
        P("leaf", None),
        P("leaf", None),
        P(),
        P(),
    )
    return jax.shard_map(
        body, mesh=mesh, in_specs=placed, out_specs=P("leaf", None, "rhs"), check_vma=False
    )
```

profile of v0, /device:TPU:32, one launch (start us, length us, event | category | flops | bytes accessed | tf_op | source)
XLA Modules:
  0.0 800.3 jit_solution(15647323932829310956)
XLA Ops:
  6.5 0.7 all-gather.2.cloned.1.call-update
  7.3 0.7 copy-done.2
  7.9 2.6 convolution_convert_fusion
  10.5 1.4 fusion.33
  11.9 3.8 collective-permute-start.4
  15.6 1.3 collective-permute-start.5
  16.9 6.1 collective-permute-start.2
  23.0 3.1 collective-permute-start.3
  26.1 3.8 collective-permute-start
  30.1 1.1 broadcast_multiply_fusion
  31.5 685.1 %all-reduce.1 = bf16[16,128,128]{1,2,0:T(8,128)(2,1)S(1)} all-reduce(f32[16,128,128]{1,2,0:T(8,128)} %broadcast_multiply_fusion), channel_id=1, replica_groups=mesh['leaf'=128,'rhs'=2] {'leaf'}, use_global_device_ids=true, to_apply=%region_0.1 | all-reduce | flops 262144 | bytes 1572864 | tf_op jit(solution)/shard_map/psum | solution.py:112
  716.6 2.1 gather_fusion.1
  719.6 0.6 gather_fusion.2
  720.2 0.7 subtract_bitcast_fusion
  720.9 0.3 fusion.32
  721.2 2.5 fusion.60
  723.8 1.4 fusion.61
  725.2 1.8 fusion.14
  727.2 9.6 %collective-permute-start.1 = (bf16[16,128,128]{2,1,0:T(8,128)(2,1)}, bf16[16,128,128]{2,1,0:T(8,128)(2,1)S(1)}, u32[]{:S(2)}, u32[]{:S(2)}) collective-permute-start(bf16[16,128,128]{2,1,0:T(8,128)(2,1)} %convolution_convert_fusion), channel_id=1, source_target_pairs={{2,0},{4,2},{6,4},{8,6},{10,8},{12,10},{14,12},{16,14},{18,16},{20... | collective-permute-start | bytes 1572872 | tf_op jit(solution)/shard_map/ppermute | solution.py:24
  736.8 1.9 collective-permute-start.6
  738.8 4.9 collective-permute-start.7
  743.7 0.8 pad_maximum_fusion.2
  745.2 2.3 convolution_bitcast_fusion
  747.5 1.4 pad_maximum_fusion.1
  748.9 3.0 gather_fusion
  751.9 6.4 copy.41
  758.3 1.4 pad_maximum_fusion
  759.7 6.0 gather_fusion.3
  765.7 8.7 %copy.51 = bf16[16,6,256,128]{2,3,1,0:T(8,128)(2,1)} copy(bf16[16,6,256,128]{3,2,1,0:T(8,128)(2,1)} %bitcast.88) | data formatting | bytes 12582912 | tf_op jit(solution)/shard_map/jit(_take)/gather | solution.py:89
  774.4 6.4 fusion.30
  780.8 11.3 %fusion.17 = bf16[16,256,128]{1,2,0:T(8,128)(2,1)S(1)} fusion(f32[16,128,256]{2,1,0:T(8,128)} %fusion.30, bf16[16,6,256,256]{3,2,1,0:T(8,128)(2,1)} %all-gather.2.cloned.1.call-done, bf16[16,6,256,128]{2,3,1,0:T(8,128)(2,1)} %copy.51, pred[16,6]{1,0:T(8,128)(4,1)S(1)} %copy.49), kind=kOutput, calls=%fused_computation.21 | convolution fusion | flops 1614807040 | bytes 22020192 | tf_op jit(solution)/shard_map/gsab,gsbc->gac/dot_general | solution.py:90
  792.1 1.3 copy.52
  (72 shorter events, 2.2 us)
Async XLA Ops:
  6.5 718.7 %copy-start = (bf16[16,4,128,128]{3,2,1,0:T(8,128)(2,1)S(1)}, bf16[16,4,128,128]{3,2,1,0:T(8,128)(2,1)}, u32[]{:S(2)}) copy-start(bf16[16,4,128,128]{3,2,1,0:T(8,128)(2,1)} %param.23) | copy-start | bytes 6291460
  6.5 1.4 copy-start.2
  6.5 774.3 %all-gather.2.cloned.1.call-start = ((), (), s32[]{:S(2)}) async-start(), calls=%async_computation | async-start | bytes 18874368 | tf_op jit(solution)/shard_map/all_gather | solution.py:92
  7.9 2.6 copy-start.6
  7.9 22.0 %copy-start.10 = (bf16[1,128,128]{2,1,0:T(8,128)(2,1)S(1)}, bf16[1,128,128]{2,1,0:T(8,128)(2,1)}, u32[]{:S(2)}) copy-start(bf16[1,128,128]{2,1,0:T(8,128)(2,1)} %param.19) | copy-start | bytes 98308
  7.9 23.3 %copy-start.13 = (s32[16,4]{0,1:T(4,128)S(1)}, s32[16,4]{0,1:T(4,128)}, u32[]{:S(2)}) copy-start(s32[16,4]{0,1:T(4,128)} %param.29) | copy-start | bytes 772
  11.9 715.4 %collective-permute-start.4 = (bf16[128,128]{0,1:T(8,128)(2,1)S(1)}, bf16[128,128]{0,1:T(8,128)(2,1)S(1)}, u32[]{:S(2)}, u32[]{:S(2)}) collective-permute-start(bf16[128,128]{0,1:T(8,128)(2,1)S(1)} %bitcast.92), channel_id=1, source_target_pairs={{2,0},{4,2},{6,4},{8,6},{10,8},{12,10},{14,12},{16,14},{18,16},{20... | collective-permute-start | bytes 98312 | tf_op jit(solution)/shard_map/ppermute | solution.py:13
  15.6 721.2 %collective-permute-start.5 = (bf16[128,128]{0,1:T(8,128)(2,1)S(1)}, bf16[128,128]{0,1:T(8,128)(2,1)S(1)}, u32[]{:S(2)}, u32[]{:S(2)}) collective-permute-start(bf16[128,128]{0,1:T(8,128)(2,1)S(1)} %bitcast.93), channel_id=1, source_target_pairs={{4,0},{6,2},{8,4},{10,6},{12,8},{14,10},{16,12},{18,14},{20,16},{2... | collective-permute-start | bytes 98312 | tf_op jit(solution)/shard_map/ppermute | solution.py:13
  16.9 721.8 %collective-permute-start.2 = (bf16[128,128]{0,1:T(8,128)(2,1)S(1)}, bf16[128,128]{0,1:T(8,128)(2,1)}, u32[]{:S(2)}, u32[]{:S(2)}) collective-permute-start(bf16[128,128]{0,1:T(8,128)(2,1)S(1)} %bitcast.94), channel_id=1, source_target_pairs={{0,4},{2,6},{4,8},{6,10},{8,12},{10,14},{12,16},{14,18},{16,20},{1... | collective-permute-start | bytes 98312 | tf_op jit(solution)/shard_map/ppermute | solution.py:13
  23.0 720.7 %collective-permute-start.3 = (bf16[128,128]{0,1:T(8,128)(2,1)S(1)}, bf16[128,128]{0,1:T(8,128)(2,1)}, u32[]{:S(2)}, u32[]{:S(2)}) collective-permute-start(bf16[128,128]{0,1:T(8,128)(2,1)S(1)} %bitcast.95), channel_id=1, source_target_pairs={{0,2},{2,4},{4,6},{6,8},{8,10},{10,12},{12,14},{14,16},{16,18},{18... | collective-permute-start | bytes 98312 | tf_op jit(solution)/shard_map/ppermute | solution.py:13
  26.1 721.4 %collective-permute-start = (bf16[16,128,128]{2,1,0:T(8,128)(2,1)}, bf16[16,128,128]{2,1,0:T(8,128)(2,1)}, u32[]{:S(2)}, u32[]{:S(2)}) collective-permute-start(bf16[16,128,128]{2,1,0:T(8,128)(2,1)} %convolution_convert_fusion), channel_id=1, source_target_pairs={{0,2},{2,4},{4,6},{6,8},{8,10},{10,12},{12,14},{14,16},{16,18},{18... | collective-permute-start | bytes 1572872 | tf_op jit(solution)/shard_map/ppermute | solution.py:21
  716.6 2.2 copy-start.5
  716.6 2.6 copy-start.14
  716.6 2.8 copy-start.15
  716.6 3.0 copy-start.16
  716.6 4.3 copy-start.11
  721.2 4.0 copy-start.4
  725.2 19.4 %copy-start.17 = (s32[4]{0:T(128)S(1)}, s32[4]{0:T(128)}, u32[]{:S(2)}) copy-start(s32[4]{0:T(128)} %constant.92.clone) | copy-start | bytes 52
  725.2 19.7 %copy-start.12 = (bf16[1,4,128,128]{3,2,1,0:T(8,128)(2,1)S(1)}, bf16[1,4,128,128]{3,2,1,0:T(8,128)(2,1)}, u32[]{:S(2)}) copy-start(bf16[1,4,128,128]{3,2,1,0:T(8,128)(2,1)} %param.22) | copy-start | bytes 393220
  725.2 19.9 %copy-start.7 = (bf16[16,128,128]{2,1,0:T(8,128)(2,1)S(1)}, bf16[16,128,128]{2,1,0:T(8,128)(2,1)}, u32[]{:S(2)}) copy-start(bf16[16,128,128]{2,1,0:T(8,128)(2,1)} %param.18) | copy-start | bytes 1572868
  727.2 20.3 %collective-permute-start.1 = (bf16[16,128,128]{2,1,0:T(8,128)(2,1)}, bf16[16,128,128]{2,1,0:T(8,128)(2,1)S(1)}, u32[]{:S(2)}, u32[]{:S(2)}) collective-permute-start(bf16[16,128,128]{2,1,0:T(8,128)(2,1)} %convolution_convert_fusion), channel_id=1, source_target_pairs={{2,0},{4,2},{6,4},{8,6},{10,8},{12,10},{14,12},{16,14},{18,16},{20... | collective-permute-start | bytes 1572872 | tf_op jit(solution)/shard_map/ppermute | solution.py:24
  736.8 21.4 %collective-permute-start.6 = (bf16[8,256,128]{2,1,0:T(8,128)(2,1)}, bf16[8,256,128]{2,1,0:T(8,128)(2,1)}, u32[]{:S(2)}, u32[]{:S(2)}) collective-permute-start(bf16[8,256,128]{2,1,0:T(8,128)(2,1)} %get-tuple-element.9), channel_id=1, source_target_pairs={{0,2},{2,4},{4,6},{6,8},{8,10},{10,12},{12,14},{14,16},{16,18},{18... | collective-permute-start | bytes 1572872 | tf_op jit(solution)/shard_map/ppermute | solution.py:21
  738.8 19.5 %collective-permute-start.7 = (bf16[8,256,128]{2,1,0:T(8,128)(2,1)}, bf16[8,256,128]{2,1,0:T(8,128)(2,1)}, u32[]{:S(2)}, u32[]{:S(2)}) collective-permute-start(bf16[8,256,128]{2,1,0:T(8,128)(2,1)} %get-tuple-element.10), channel_id=1, source_target_pairs={{2,0},{4,2},{6,4},{8,6},{10,8},{12,10},{14,12},{16,14},{18,16},{20... | collective-permute-start | bytes 1572872 | tf_op jit(solution)/shard_map/ppermute | solution.py:24
  751.9 6.4 copy-start.3
  765.7 8.7 %copy-start.8 = (bf16[16,256,128]{2,1,0:T(8,128)(2,1)S(1)}, bf16[16,256,128]{2,1,0:T(8,128)(2,1)}, u32[]{:S(2)}) copy-start(bf16[16,256,128]{2,1,0:T(8,128)(2,1)} %param.17) | copy-start | bytes 3145732
  765.7 8.7 %copy-start.9 = (f32[16,128,128]{1,2,0:T(8,128)S(1)}, f32[16,128,128]{1,2,0:T(8,128)}, u32[]{:S(2)}) copy-start(f32[16,128,128]{1,2,0:T(8,128)} %convolution_bitcast_fusion) | copy-start | bytes 3145732
  780.8 12.6 %copy-start.1 = (bf16[16,4,128,128]{3,2,1,0:T(8,128)(2,1)S(1)}, bf16[16,4,128,128]{3,2,1,0:T(8,128)(2,1)}, u32[]{:S(2)}) copy-start(bf16[16,4,128,128]{3,2,1,0:T(8,128)(2,1)} %param.23) | copy-start | bytes 6291460
Sparse Core Ops, SparseCore 0:
  9.2 32.5 all-gather.1
where the time goes:
time: 801 us; the launch traced here: 800 us
  blocking collectives  685 us (86%)
  starting transfers between devices  34.4 us (4%)
  local copies, waits for them, and re-layouts  32.4 us (4%)
  matrix products  28.4 us (4%)
  between operations  13.8 us (2%)
    psum x1, blocking collectives, body(): moments1 = lax.psum(placed, 'leaf').astype(jnp.bfloat16)  685 us
  transfers between devices with their start and end apart: 9, of which 0 were waited for; matrix products, arithmetic and copies ran while one was open for 7% of the time, Pallas kernels for 0%

commit v1 on v0

v1 whole, which is shorter than its diff:
```python
import functools

import jax
import jax.numpy as jnp
from jax import lax
from jax.experimental import pallas as pl
from jax.experimental.pallas import tpu as pltpu
from jax.sharding import Mesh, PartitionSpec as P

TOP1 = 16
TOP0 = 4
FAN = TOP1 // TOP0
LEAF = ("y", "x", "z")
F32 = jnp.float32
BF16 = jnp.bfloat16
VMEM_LIMIT = 48 * 1024 * 1024


def dot(a, b):
    return lax.dot_general(a, b, (((1,), (0,)), ((), ())), preferred_element_type=F32)


def dot_t(a, b):
    return lax.dot_general(a, b, (((0,), (0,)), ((), ())), preferred_element_type=F32)


def shifted(block, distance):
    devices = range(lax.axis_size(LEAF))
    route = [(i - distance, i) for i in devices if i - distance in devices]
    return lax.ppermute(block, LEAF, route)


def moments_kernel(steps, per, basis, charges, transfer3, transfer2, message, spread, total):
    step = pl.program_id(0)
    share = jnp.zeros(total.shape, F32)
    for i in range(per):
        moment = dot_t(basis[i], charges[i]).astype(BF16)
        message[step * per + i] = moment
        share = share + dot_t(transfer3[i], moment)

    @pl.when(step == 0)
    def _():
        total[...] = share

    @pl.when(step > 0)
    def _():
        total[...] = total[...] + share

    @pl.when(step == steps - 1)
    def _():
        moment2 = total[...].astype(BF16)
        message[steps * per] = moment2
        term = dot_t(transfer2[0], moment2).astype(BF16)
        for i in range(spread.shape[0]):
            spread[i] = term


def moments(charges, basis, transfer3, transfer2):
    leaves, box, width = charges.shape
    rank = basis.shape[2]
    per = 4
    steps = leaves // per
    return pl.pallas_call(
        functools.partial(moments_kernel, steps, per),
        grid=(steps,),
        in_specs=[
            pl.BlockSpec((per, box, rank), lambda i: (i, 0, 0)),
            pl.BlockSpec((per, box, width), lambda i: (i, 0, 0)),
            pl.BlockSpec((per, rank, rank), lambda i: (i, 0, 0)),
            pl.BlockSpec((1, rank, rank), lambda i: (0, 0, 0)),
        ],
        out_specs=[
            pl.BlockSpec((leaves + 1, rank, width), lambda i: (0, 0, 0)),
            pl.BlockSpec((TOP1, rank, width), lambda i: (0, 0, 0)),
        ],
        out_shape=[
            jax.ShapeDtypeStruct((leaves + 1, rank, width), BF16),
            jax.ShapeDtypeStruct((TOP1, rank, width), BF16),
        ],
        scratch_shapes=[pltpu.VMEM((rank, width), F32)],
        compiler_params=pltpu.CompilerParams(vmem_limit_bytes=VMEM_LIMIT),
        cost_estimate=pl.CostEstimate(
            flops=2 * leaves * rank * width * (box + rank),
            bytes_accessed=4 * 1024 * 1024,
            transcendentals=0,
        ),
        name="moments",
    )(basis, charges, transfer3, transfer2)


def leaves_kernel(
    near_list,
    far_list,
    low,
    own,
    high,
    message_low,
    message,
    message_high,
    mine,
    theirs,
    coupling,
    near,
    far,
    sources,
    moment_sources,
    near_sems,
    far_sems,
):
    step = pl.program_id(0)
    half = low.shape[0]
    count = own.shape[0]
    first = (lax.axis_index("y") * lax.axis_size("x") + lax.axis_index("x")) * lax.axis_size(
        "z"
    ) + lax.axis_index("z")
    first = first * count
    core = lax.axis_index("core")

    near_copies = [
        pltpu.make_async_copy(low, sources.at[pl.ds(0, half)], near_sems.at[0]),
        pltpu.make_async_copy(own, sources.at[pl.ds(half, count)], near_sems.at[1]),
        pltpu.make_async_copy(high, sources.at[pl.ds(half + count, half)], near_sems.at[2]),
    ]
    far_copies = [
        pltpu.make_async_copy(
            part.at[pl.ds(0, count)], moment_sources.at[pl.ds(place * count, count)], far_sems.at[place]
        )
        for place, part in enumerate((message_low, message, message_high))
    ]

    @pl.when(step == 0)
    def _():
        for copy in near_copies + far_copies:
            copy.start()
        for copy in near_copies:
            copy.wait()

    blocks = mine.shape[1]
    left = jnp.concatenate(
        [mine[0, s] for s in range(blocks)] + [theirs[0, s] for s in range(blocks)], axis=1
    )
    places = [near_list[step, core * blocks + s] for s in range(blocks)] + [
        near_list[step, (1 - core) * blocks + s] for s in range(blocks)
    ]
    right = jnp.concatenate([sources[place - first + half] for place in places], axis=0)
    near[0] = dot(left, right)

    @pl.when(step == 0)
    def _():
        for copy in far_copies:
            copy.wait()

    partners = coupling.shape[1]
    left = jnp.concatenate([coupling[0, f] for f in range(partners)], axis=1)
    right = jnp.concatenate(
        [moment_sources[far_list[step, f] - first + count] for f in range(partners)], axis=0
    )
    far[0] = dot(left, right)


def leaf_parts(
    near_list, far_list, low, own, high, message_low, message, message_high, mine, theirs, coupling
):
    leaves, box, width = own.shape
    half = low.shape[0]
    blocks = mine.shape[1]
    partners, rank = coupling.shape[1], coupling.shape[2]
    anywhere = pl.BlockSpec(memory_space=pl.ANY)
    return pl.pallas_call(
        leaves_kernel,
        grid_spec=pltpu.PrefetchScalarGridSpec(
            num_scalar_prefetch=2,
            grid=(leaves,),
            in_specs=[anywhere] * 6
            + [
                pl.BlockSpec((1, blocks, box, box), lambda i, *_: (i, 0, 0, 0)),
                pl.BlockSpec((1, blocks, box, box), lambda i, *_: (i, 0, 0, 0)),
                pl.BlockSpec((1, partners, rank, rank), lambda i, *_: (i, 0, 0, 0)),
            ],
            out_specs=[
                pl.BlockSpec((1, box, width), lambda i, *_: (i, 0, 0)),
                pl.BlockSpec((1, rank, width), lambda i, *_: (i, 0, 0)),
            ],
            scratch_shapes=[
                pltpu.VMEM((leaves + 2 * half, box, width), BF16),
                pltpu.VMEM((3 * leaves, rank, width), BF16),
                pltpu.SemaphoreType.DMA((3,)),
                pltpu.SemaphoreType.DMA((3,)),
            ],
        ),
        out_shape=[
            jax.ShapeDtypeStruct((leaves, box, width), F32),
            jax.ShapeDtypeStruct((leaves, rank, width), F32),
        ],
        compiler_params=pltpu.CompilerParams(vmem_limit_bytes=VMEM_LIMIT),
        cost_estimate=pl.CostEstimate(
            flops=2 * leaves * width * (2 * blocks * box * box + partners * rank * rank),
            bytes_accessed=24 * 1024 * 1024,
            transcendentals=0,
        ),
        name="leaf_parts",
    )(near_list, far_list, low, own, high, message_low, message, message_high, mine, theirs, coupling)


def upper_kernel(far1, far0, terms, below, transfer1, coupling1, coupling0, spread):
    node = lax.axis_index("y") * lax.axis_size("x") + lax.axis_index("x")
    root = node // FAN
    source = far0[root]
    top = jnp.zeros(spread.shape[1:], F32)
    for i in range(FAN):
        top = top + dot_t(below[i], terms[source * FAN + i])
    local0 = dot(coupling0[0], top.astype(BF16)).astype(BF16)
    total = dot(transfer1[0], local0)
    for f in range(coupling1.shape[1]):
        total = total + dot(coupling1[0, f], terms[far1[node, f]])
    total = total.astype(BF16)
    for i in range(spread.shape[0]):
        spread[i] = total


def upper(far1, far0, terms, transfer1, coupling1, coupling0):
    count, rank, width = terms.shape
    partners = coupling1.shape[1]
    fellows = lax.axis_size("z")

    def node():
        return lax.axis_index("y") * lax.axis_size("x") + lax.axis_index("x")

    return pl.pallas_call(
        upper_kernel,
        grid_spec=pltpu.PrefetchScalarGridSpec(
            num_scalar_prefetch=2,
            grid=(1,),
            in_specs=[
                pl.BlockSpec((count, rank, width), lambda i, *_: (0, 0, 0)),
                pl.BlockSpec((FAN, rank, rank), lambda i, far1, far0: (far0[node() // FAN], 0, 0)),
                pl.BlockSpec((1, rank, rank), lambda i, *_: (node(), 0, 0)),
                pl.BlockSpec((1, partners, rank, rank), lambda i, *_: (node(), 0, 0, 0)),
                pl.BlockSpec((1, rank, rank), lambda i, *_: (node() // FAN, 0, 0)),
            ],
            out_specs=pl.BlockSpec((fellows, rank, width), lambda i, *_: (0, 0, 0)),
        ),
        out_shape=jax.ShapeDtypeStruct((fellows, rank, width), BF16),
        compiler_params=pltpu.CompilerParams(vmem_limit_bytes=VMEM_LIMIT),
        cost_estimate=pl.CostEstimate(
            flops=2 * 10 * rank * rank * width, bytes_accessed=1024 * 1024, transcendentals=0
        ),
        name="upper",
    )(far1, far0, terms, transfer1, transfer1, coupling1, coupling0)


def finish_kernel(
    per,
    far2,
    pieces,
    down1,
    up1,
    down2,
    up2,
    transfer2,
    coupling2,
    basis,
    transfer3,
    near,
    far,
    potential,
    local2,
):
    step = pl.program_id(0)

    @pl.when(step == 0)
    def _():
        total = pieces[0].astype(F32)
        for i in range(1, pieces.shape[0]):
            total = total + pieces[i].astype(F32)
        result = dot(transfer2[0], total.astype(BF16))
        device = (lax.axis_index("y") * lax.axis_size("x") + lax.axis_index("x")) * lax.axis_size(
            "z"
        ) + lax.axis_index("z")
        for f in range(coupling2.shape[1]):
            offset = far2[0, f] - device
            source = jnp.where(
                offset < 0,
                jnp.where(offset == -1, down1[0], down2[...]),
                jnp.where(offset == 1, up1[0], up2[...]),
            )
            result = result + dot(coupling2[0, f], source)
        local2[...] = result.astype(BF16)

    parent = local2[...]
    for i in range(per):
        local3 = (far[i] + dot(transfer3[i], parent)).astype(BF16)
        potential[i] = (near[i] + dot(basis[i], local3)).astype(BF16)


def finish(far2, pieces, down1, up1, down2, up2, transfer2, coupling2, basis, transfer3, near, far):
    leaves, box, width = near.shape
    rank = far.shape[1]
    partners = coupling2.shape[1]
    per = 4
    fixed = lambda i, *_: (0, 0, 0)
    along = lambda i, *_: (i, 0, 0)
    last = lambda i, *_: (leaves, 0, 0)
    return pl.pallas_call(
        functools.partial(finish_kernel, per),
        grid_spec=pltpu.PrefetchScalarGridSpec(
            num_scalar_prefetch=1,
            grid=(leaves // per,),
            in_specs=[
                pl.BlockSpec(pieces.shape, fixed),
                pl.BlockSpec((1, rank, width), last),
                pl.BlockSpec((1, rank, width), last),
                pl.BlockSpec((rank, width), lambda i, *_: (0, 0)),
                pl.BlockSpec((rank, width), lambda i, *_: (0, 0)),
                pl.BlockSpec((1, rank, rank), fixed),
                pl.BlockSpec((1, partners, rank, rank), lambda i, *_: (0, 0, 0, 0)),
                pl.BlockSpec((per, box, rank), along),
                pl.BlockSpec((per, rank, rank), along),
                pl.BlockSpec((per, box, width), along),
                pl.BlockSpec((per, rank, width), along),
            ],
            out_specs=pl.BlockSpec((per, box, width), along),
            scratch_shapes=[pltpu.VMEM((rank, width), BF16)],
        ),
        out_shape=jax.ShapeDtypeStruct((leaves, box, width), BF16),
        compiler_params=pltpu.CompilerParams(vmem_limit_bytes=VMEM_LIMIT),
        cost_estimate=pl.CostEstimate(
            flops=2 * leaves * rank * width * (box + rank),
            bytes_accessed=6 * 1024 * 1024,
            transcendentals=0,
        ),
        name="finish",
    )(far2, pieces, down1, up1, down2, up2, transfer2, coupling2, basis, transfer3, near, far)


def body(
    charges,
    leaf_basis,
    transfer3,
    transfer2,
    transfer1,
    coupling3,
    coupling2,
    coupling1,
    coupling0,
    near_blocks,
    near_list,
    far_list3,
    far_list2,
    far_list1,
    far_list0,
):
    leaves = charges.shape[0]
    half = leaves // 2
    other_blocks = lax.ppermute(near_blocks, "core", [(0, 1), (1, 0)])
    low = shifted(charges[leaves - half :], 1)
    high = shifted(charges[:half], -1)
    message, spread = moments(charges, leaf_basis, transfer3, transfer2)
    terms = lax.all_to_all(spread, ("y", "x"), 0, 0, tiled=True)
    message_low = shifted(message, 1)
    message_high = shifted(message, -1)
    down2 = shifted(message[leaves], 2)
    up2 = shifted(message[leaves], -2)
    near, far = leaf_parts(
        near_list,
        far_list3,
        low,
        charges,
        high,
        message_low,
        message,
        message_high,
        near_blocks,
        other_blocks,
        coupling3,
    )
    pieces = upper(far_list1, far_list0, terms, transfer1, coupling1, coupling0)
    pieces = lax.all_to_all(pieces, "z", 0, 0, tiled=True)
    return finish(
        far_list2,
        pieces,
        message_low,
        message_high,
        down2,
        up2,
        transfer2,
        coupling2,
        leaf_basis,
        transfer3,
        near,
        far,
    )


def solution(mesh):
    grid = Mesh(mesh.devices.reshape(4, 4, 8, 2), ("y", "x", "z", "core"))
    placed = (
        P(LEAF, None, "core"),
        P(LEAF, None, None),
        P(LEAF, None, None),
        P(LEAF, None, None),
        P(),
        P(LEAF, None, None, None),
        P(LEAF, None, None, None),
        P(),
        P(),
        P(LEAF, "core", None, None),
        P(LEAF, None),
        P(LEAF, None),
        P(LEAF, None),
        P(),
        P(),
    )
    return jax.shard_map(
        body, mesh=grid, in_specs=placed, out_specs=P(LEAF, None, "core"), check_vma=False
    )
```

time: 801 us -> 105 us (0.13)
  the two profiles are of different devices: /device:TPU:32 before, /device:TPU:10 now
where the time goes in v1:
time: 105 us; the launch traced here: 103 us
  starting transfers between devices  54.8 us (52%)
  Pallas kernels  28.1 us (27%)
  local copies, waits for them, and re-layouts  14.9 us (14%)
  waiting for transfers between devices  5.31 us (5%)
    ppermute x6, starting transfers between devices, shifted(): return lax.ppermute(block, LEAF, route)  36.6 us
    pallas_call x1, Pallas kernels, leaf_parts(): pl.pallas_call(leaves_kernel, grid_spec=pltpu.PrefetchScalarGridSpec(num_...  18 us
    unnamed x47, local copies, waits for them, and re-layouts  13.1 us
    all_to_all x1, starting transfers between devices, body(): pieces = lax.all_to_all(pieces, 'z', 0, 0, tiled=True)  10.8 us
    all_to_all x1, starting transfers between devices, body(): terms = lax.all_to_all(spread, ('y', 'x'), 0, 0, tiled=True)  7.41 us
    pallas_call x1, Pallas kernels, finish(): pl.pallas_call(functools.partial(finish_kernel, per), grid_spec=pltpu.Pre...  5.3 us
    all_to_all x1, waiting for transfers between devices, body(): terms = lax.all_to_all(spread, ('y', 'x'), 0, 0, tiled=True)  5.29 us
    pallas_call x1, Pallas kernels, moments(): pl.pallas_call(functools.partial(moments_kernel, steps, per), grid=(steps...  2.76 us
  transfers between devices with their start and end apart: 9, of which 1 were waited for; matrix products, arithmetic and copies ran while one was open for 2% of the time, Pallas kernels for 22%

profile of v1, /device:TPU:10, one launch (start us, length us, event | category | flops | bytes accessed | tf_op | source)
XLA Modules:
  0.0 103.2 jit_solution(12094914346527952576)
XLA Ops:
  0.0 1.2 %copy-done = bf16[16,256,128]{2,1,0:T(8,128)(2,1)S(1)} copy-done((bf16[16,256,128]{2,1,0:T(8,128)(2,1)S(1)}, bf16[16,256,128]{2,1,0:T(8,128)(2,1)}, u32[]{:S(2)}) %copy-start) | copy-done | bytes 1048600
  1.2 1.2 %copy-done.2 = bf16[16,256,128]{2,1,0:T(8,128)(2,1)S(1)} copy-done((bf16[16,256,128]{2,1,0:T(8,128)(2,1)S(1)}, bf16[16,256,128]{2,1,0:T(8,128)(2,1)}, u32[]{:S(2)}) %copy-start.2) | copy-done | bytes 1048600
  2.5 1.0 %copy-done.6 = bf16[16,128,128]{2,1,0:T(8,128)(2,1)S(1)} copy-done((bf16[16,128,128]{2,1,0:T(8,128)(2,1)S(1)}, bf16[16,128,128]{2,1,0:T(8,128)(2,1)}, u32[]{:S(2)}) %copy-start.6) | copy-done | bytes 524312
  3.5 0.8 copy-done.12
  4.3 2.8 %moments.1 = (bf16[17,128,128]{2,1,0:T(8,128)(2,1)}, bf16[16,128,128]{2,1,0:T(8,128)(2,1)S(1)}) custom-call(bf16[16,256,128]{2,1,0:T(8,128)(2,1)S(1)} %copy-done.2, bf16[16,256,128]{2,1,0:T(8,128)(2,1)S(1)} %copy-done, bf16[16,128,128]{2,1,0:T(8,128)(2,1)S(1)} %copy-done.6, bf16[1,128,128]{2,1,0:T(8,128)(2,1)S(1)} %copy-done.12), custom_call_target="tpu_custom_call" | custom-call | flops 201326592 | bytes 4194304 | tf_op jit(solution)/shard_map/moments/pallas_call | solution.py:63
  7.0 0.8 copy-done.10
  7.9 7.9 %collective-permute-start.1 = (bf16[17,128,128]{2,1,0:T(8,128)(2,1)}, bf16[17,128,128]{2,1,0:T(8,128)(2,1)S(1)}, u32[]{:S(2)}, u32[]{:S(2)}) collective-permute-start(bf16[17,128,128]{2,1,0:T(8,128)(2,1)} %get-tuple-element.10.message), channel_id=1, source_target_pairs={{2,0},{4,2},{6,4},{8,6},{10,8},{12,10},{14,12},{16,14},{18,16},{20... | collective-permute-start | bytes 1671176 | tf_op jit(solution)/shard_map/ppermute | solution.py:30
  15.7 1.9 %collective-permute-start = (bf16[17,128,128]{2,1,0:T(8,128)(2,1)}, bf16[17,128,128]{2,1,0:T(8,128)(2,1)S(1)}, u32[]{:S(2)}, u32[]{:S(2)}) collective-permute-start(bf16[17,128,128]{2,1,0:T(8,128)(2,1)} %get-tuple-element.10.message), channel_id=1, source_target_pairs={{0,2},{2,4},{4,6},{6,8},{8,10},{10,12},{12,14},{14,16},{16,18},{18... | collective-permute-start | bytes 1671176 | tf_op jit(solution)/shard_map/ppermute | solution.py:30
  17.7 7.4 %all-to-all-start = ((bf16[16,128,128]{2,1,0:T(8,128)(2,1)}), bf16[16,128,128]{2,1,0:T(8,128)(2,1)S(1)}, u32[]{:S(2)}, u32[]{:S(2)}) async-start(bf16[16,128,128]{2,1,0:T(8,128)(2,1)} %copy-done.10), calls=%async_computation | async-start | bytes 1048576 | tf_op jit(solution)/shard_map/all_to_all | solution.py:359
  25.1 1.1 %fusion = (bf16[8,256,128]{2,1,0:T(8,128)(2,1)}, bf16[8,256,128]{2,1,0:T(8,128)(2,1)}) fusion(bf16[16,256,128]{2,1,0:T(8,128)(2,1)S(1)} %copy-done.1), kind=kLoop, calls=%fused_computation.1 | loop fusion | bytes 2097152 | tf_op jit(solution)/shard_map/slice | solution.py:357
  26.1 7.9 %collective-permute-start.5 = (bf16[8,256,128]{2,1,0:T(8,128)(2,1)}, bf16[8,256,128]{2,1,0:T(8,128)(2,1)}, u32[]{:S(2)}, u32[]{:S(2)}) collective-permute-start(bf16[8,256,128]{2,1,0:T(8,128)(2,1)} %get-tuple-element.13), channel_id=1, source_target_pairs={{2,0},{4,2},{6,4},{8,6},{10,8},{12,10},{14,12},{16,14},{18,16},{20... | collective-permute-start | bytes 1572872 | tf_op jit(solution)/shard_map/ppermute | solution.py:30
  34.0 1.9 %collective-permute-start.4 = (bf16[8,256,128]{2,1,0:T(8,128)(2,1)}, bf16[8,256,128]{2,1,0:T(8,128)(2,1)}, u32[]{:S(2)}, u32[]{:S(2)}) collective-permute-start(bf16[8,256,128]{2,1,0:T(8,128)(2,1)} %get-tuple-element.14), channel_id=1, source_target_pairs={{0,2},{2,4},{4,6},{6,8},{8,10},{10,12},{12,14},{14,16},{16,18},{18... | collective-permute-start | bytes 1572872 | tf_op jit(solution)/shard_map/ppermute | solution.py:30
  36.0 0.1 copy.16.far1
  36.0 5.3 %all-to-all-done.terms = bf16[16,128,128]{2,1,0:T(8,128)(2,1)S(1)} async-done(((bf16[16,128,128]{2,1,0:T(8,128)(2,1)}), bf16[16,128,128]{2,1,0:T(8,128)(2,1)S(1)}, u32[]{:S(2)}, u32[]{:S(2)}) %all-to-all-start) | async-done | bytes 524320 | tf_op jit(solution)/shard_map/all_to_all | solution.py:359
  41.3 0.0 copy-start.5
  41.3 1.6 %copy-done.5 = bf16[16,4,128,128]{3,2,1,0:T(8,128)(2,1)S(1)} copy-done((bf16[16,4,128,128]{3,2,1,0:T(8,128)(2,1)S(1)}, bf16[16,4,128,128]{3,2,1,0:T(8,128)(2,1)}, u32[]{:S(2)}) %copy-start.5) | copy-done | bytes 2097176
  42.9 2.0 %upper.1 = bf16[8,128,128]{2,1,0:T(8,128)(2,1)} custom-call(s32[16,4]{1,0:T(8,128)S(1)} %copy.16.far1, s32[4]{0:T(128)S(1)} %copy-done.17, bf16[16,128,128]{2,1,0:T(8,128)(2,1)S(1)} %all-to-all-done.terms, bf16[16,128,128]{2,1,0:T(8,128)(2,1)S(1)} %copy-done.4, bf16[16,128,128]{2,1,0:T(8,128)(2,1)S(1)} %copy-done.4, bf16[16,4,128,128]{3,2,1,0:T(8,128)(2,1)S(1)} %copy-done.5, ...), custom_call_target="tpu_custom_call" | custom-call | flops 41943040 | bytes 1048576 | tf_op jit(solution)/shard_map/upper/pallas_call | solution.py:229
  44.9 10.8 %all-to-all-start.1 = ((bf16[8,128,128]{2,1,0:T(8,128)(2,1)}), bf16[8,128,128]{2,1,0:T(8,128)(2,1)S(1)}, u32[]{:S(2)}, u32[]{:S(2)}) async-start(bf16[8,128,128]{2,1,0:T(8,128)(2,1)} %upper.1), calls=%async_computation.1 | async-start | bytes 524288 | tf_op jit(solution)/shard_map/all_to_all | solution.py:378
  55.7 0.1 copy.17.near_list
  55.8 0.1 copy.18.far_list
  55.8 0.8 slice_bitcast_fusion
  56.6 15.1 %collective-permute-start.3 = (bf16[128,128]{1,0:T(8,128)(2,1)S(1)}, bf16[128,128]{1,0:T(8,128)(2,1)S(1)}, u32[]{:S(2)}, u32[]{:S(2)}) collective-permute-start(bf16[128,128]{1,0:T(8,128)(2,1)S(1)} %slice_bitcast_fusion), channel_id=1, source_target_pairs={{4,0},{6,2},{8,4},{10,6},{12,8},{14,10},{16,12},{18,14},{20,16},{2... | collective-permute-start | bytes 98312 | tf_op jit(solution)/shard_map/ppermute | solution.py:30
  71.8 1.9 %collective-permute-start.2 = (bf16[128,128]{1,0:T(8,128)(2,1)S(1)}, bf16[128,128]{1,0:T(8,128)(2,1)S(1)}, u32[]{:S(2)}, u32[]{:S(2)}) collective-permute-start(bf16[128,128]{1,0:T(8,128)(2,1)S(1)} %slice_bitcast_fusion), channel_id=1, source_target_pairs={{0,4},{2,6},{4,8},{6,10},{8,12},{10,14},{12,16},{14,18},{16,20},{1... | collective-permute-start | bytes 98312 | tf_op jit(solution)/shard_map/ppermute | solution.py:30
  73.7 18.0 %leaf_parts.1 = (f32[16,256,128]{2,1,0:T(8,128)}, f32[16,128,128]{2,1,0:T(8,128)S(1)}) custom-call(s32[16,6]{1,0:T(8,128)S(1)} %copy.17.near_list, s32[16,8]{1,0:T(8,128)S(1)} %copy.18.far_list, bf16[8,256,128]{2,1,0:T(8,128)(2,1)} %collective-permute-done.4.low, bf16[16,256,128]{2,1,0:T(8,128)(2,1)S(1)} %copy-done.1, ...), custom_call_target="tpu_custom_call" | custom-call | flops 2147483648 | bytes 25165824 | tf_op jit(solution)/shard_map/leaf_parts/pallas_call | solution.py:169
  91.8 1.0 copy-done.8
  92.7 0.6 copy-done.15
  93.4 1.0 %copy-done.7 = bf16[16,128,128]{2,1,0:T(8,128)(2,1)S(1)} copy-done((bf16[16,128,128]{2,1,0:T(8,128)(2,1)S(1)}, bf16[16,128,128]{2,1,0:T(8,128)(2,1)}, u32[]{:S(2)}) %copy-start.7) | copy-done | bytes 524312
  94.4 1.2 %copy-done.9 = f32[16,128,128]{2,1,0:T(8,128)S(1)} copy-done((f32[16,128,128]{2,1,0:T(8,128)S(1)}, f32[16,128,128]{2,1,0:T(8,128)}, u32[]{:S(2)}) %copy-start.9) | copy-done | bytes 1048600
  95.6 0.9 copy-done.14
  96.5 0.8 copy-done.16
  97.3 0.7 copy-done.18
  97.9 5.3 %finish.1 = bf16[16,256,128]{2,1,0:T(8,128)(2,1)} custom-call(s32[1,4]{1,0:T(1,128)S(1)} %copy-done.18, bf16[8,128,128]{2,1,0:T(8,128)(2,1)S(1)} %all-to-all-done.1.pieces, bf16[17,128,128]{2,1,0:T(8,128)(2,1)S(1)} %collective-permute-done.message_low.down1, bf16[17,128,128]{2,1,0:T(8,128)(2,1)S(1)} %collective-permute-done.1.message_high.up1, ...), custom_call_target="tpu_custom_call" | custom-call | flops 201326592 | bytes 6291456 | tf_op jit(solution)/shard_map/finish/pallas_call | solution.py:304
  (39 shorter events, 0.1 us)
Async XLA Ops:
  0.0 73.7 %collective-permute-start.6 = (bf16[16,3,256,256]{3,2,1,0:T(8,128)(2,1)}, bf16[16,3,256,256]{3,2,1,0:T(8,128)(2,1)}, u32[]{:S(2)}, u32[]{:S(2)}) collective-permute-start(bf16[16,3,256,256]{3,2,1,0:T(8,128)(2,1)} %mine.1), channel_id=1, source_target_pairs={{0,1},{1,0},{2,3},{3,2},{4,5},{5,4},{6,7},{7,6},{8,9},{9,8},{10,11... | collective-permute-start | bytes 18874376 | tf_op jit(solution)/shard_map/ppermute | solution.py:355
  0.0 1.2 %copy-start = (bf16[16,256,128]{2,1,0:T(8,128)(2,1)S(1)}, bf16[16,256,128]{2,1,0:T(8,128)(2,1)}, u32[]{:S(2)}) copy-start(bf16[16,256,128]{2,1,0:T(8,128)(2,1)} %own.1) | copy-start | bytes 3145732
  1.2 1.2 %copy-start.2 = (bf16[16,256,128]{2,1,0:T(8,128)(2,1)S(1)}, bf16[16,256,128]{2,1,0:T(8,128)(2,1)}, u32[]{:S(2)}) copy-start(bf16[16,256,128]{2,1,0:T(8,128)(2,1)} %basis.3) | copy-start | bytes 3145732
  2.5 1.0 %copy-start.6 = (bf16[16,128,128]{2,1,0:T(8,128)(2,1)S(1)}, bf16[16,128,128]{2,1,0:T(8,128)(2,1)}, u32[]{:S(2)}) copy-start(bf16[16,128,128]{2,1,0:T(8,128)(2,1)} %transfer3.3) | copy-start | bytes 1572868
  3.5 0.8 copy-start.12
  4.3 20.8 %copy-start.1 = (bf16[16,256,128]{2,1,0:T(8,128)(2,1)S(1)}, bf16[16,256,128]{2,1,0:T(8,128)(2,1)}, u32[]{:S(2)}) copy-start(bf16[16,256,128]{2,1,0:T(8,128)(2,1)} %own.1) | copy-start | bytes 3145732
  4.3 31.7 %copy-start.21 = (s32[16,4]{0,1:T(4,128)S(1)}, s32[16,4]{0,1:T(4,128)}, u32[]{:S(2)}) copy-start(s32[16,4]{0,1:T(4,128)} %param.28) | copy-start | bytes 772
  4.3 37.1 %copy-start.4 = (bf16[16,128,128]{2,1,0:T(8,128)(2,1)S(1)}, bf16[16,128,128]{2,1,0:T(8,128)(2,1)}, u32[]{:S(2)}) copy-start(bf16[16,128,128]{2,1,0:T(8,128)(2,1)} %transfer1.1) | copy-start | bytes 1572868
  4.3 37.1 %copy-start.11 = (bf16[4,128,128]{2,1,0:T(8,128)(2,1)S(1)}, bf16[4,128,128]{2,1,0:T(8,128)(2,1)}, u32[]{:S(2)}) copy-start(bf16[4,128,128]{2,1,0:T(8,128)(2,1)} %coupling0.1) | copy-start | bytes 393220
  4.3 37.1 %copy-start.17 = (s32[4]{0:T(128)S(1)}, s32[4]{0:T(128)}, u32[]{:S(2)}) copy-start(s32[4]{0:T(128)} %far0.1) | copy-start | bytes 52
  7.0 0.8 copy-start.10
  7.9 47.8 %copy-start.19 = (s32[16,6]{0,1:T(8,128)S(1)}, s32[16,6]{0,1:T(8,128)}, u32[]{:S(2)}) copy-start(s32[16,6]{0,1:T(8,128)} %param.25) | copy-start | bytes 1156
  7.9 47.9 %copy-start.20 = (s32[16,8]{0,1:T(8,128)S(1)}, s32[16,8]{0,1:T(8,128)}, u32[]{:S(2)}) copy-start(s32[16,8]{0,1:T(8,128)} %param.26) | copy-start | bytes 1540
  7.9 65.8 %collective-permute-start.1 = (bf16[17,128,128]{2,1,0:T(8,128)(2,1)}, bf16[17,128,128]{2,1,0:T(8,128)(2,1)S(1)}, u32[]{:S(2)}, u32[]{:S(2)}) collective-permute-start(bf16[17,128,128]{2,1,0:T(8,128)(2,1)} %get-tuple-element.10.message), channel_id=1, source_target_pairs={{2,0},{4,2},{6,4},{8,6},{10,8},{12,10},{14,12},{16,14},{18,16},{20... | collective-permute-start | bytes 1671176 | tf_op jit(solution)/shard_map/ppermute | solution.py:30
  15.7 58.0 %collective-permute-start = (bf16[17,128,128]{2,1,0:T(8,128)(2,1)}, bf16[17,128,128]{2,1,0:T(8,128)(2,1)S(1)}, u32[]{:S(2)}, u32[]{:S(2)}) collective-permute-start(bf16[17,128,128]{2,1,0:T(8,128)(2,1)} %get-tuple-element.10.message), channel_id=1, source_target_pairs={{0,2},{2,4},{4,6},{6,8},{8,10},{10,12},{12,14},{14,16},{16,18},{18... | collective-permute-start | bytes 1671176 | tf_op jit(solution)/shard_map/ppermute | solution.py:30
  17.7 23.7 %all-to-all-start = ((bf16[16,128,128]{2,1,0:T(8,128)(2,1)}), bf16[16,128,128]{2,1,0:T(8,128)(2,1)S(1)}, u32[]{:S(2)}, u32[]{:S(2)}) async-start(bf16[16,128,128]{2,1,0:T(8,128)(2,1)} %copy-done.10), calls=%async_computation | async-start | bytes 1048576 | tf_op jit(solution)/shard_map/all_to_all | solution.py:359
  26.1 30.5 %collective-permute-start.5 = (bf16[8,256,128]{2,1,0:T(8,128)(2,1)}, bf16[8,256,128]{2,1,0:T(8,128)(2,1)}, u32[]{:S(2)}, u32[]{:S(2)}) collective-permute-start(bf16[8,256,128]{2,1,0:T(8,128)(2,1)} %get-tuple-element.13), channel_id=1, source_target_pairs={{2,0},{4,2},{6,4},{8,6},{10,8},{12,10},{14,12},{16,14},{18,16},{20... | collective-permute-start | bytes 1572872 | tf_op jit(solution)/shard_map/ppermute | solution.py:30
  34.0 37.7 %collective-permute-start.4 = (bf16[8,256,128]{2,1,0:T(8,128)(2,1)}, bf16[8,256,128]{2,1,0:T(8,128)(2,1)}, u32[]{:S(2)}, u32[]{:S(2)}) collective-permute-start(bf16[8,256,128]{2,1,0:T(8,128)(2,1)} %get-tuple-element.14), channel_id=1, source_target_pairs={{0,2},{2,4},{4,6},{6,8},{8,10},{10,12},{12,14},{14,16},{16,18},{18... | collective-permute-start | bytes 1572872 | tf_op jit(solution)/shard_map/ppermute | solution.py:30
  41.3 1.6 %copy-start.5 = (bf16[16,4,128,128]{3,2,1,0:T(8,128)(2,1)S(1)}, bf16[16,4,128,128]{3,2,1,0:T(8,128)(2,1)}, u32[]{:S(2)}) copy-start(bf16[16,4,128,128]{3,2,1,0:T(8,128)(2,1)} %coupling1.1) | copy-start | bytes 6291460
  44.9 48.5 %all-to-all-start.1 = ((bf16[8,128,128]{2,1,0:T(8,128)(2,1)}), bf16[8,128,128]{2,1,0:T(8,128)(2,1)S(1)}, u32[]{:S(2)}, u32[]{:S(2)}) async-start(bf16[8,128,128]{2,1,0:T(8,128)(2,1)} %upper.1), calls=%async_computation.1 | async-start | bytes 524288 | tf_op jit(solution)/shard_map/all_to_all | solution.py:378
  56.6 36.8 %copy-start.3 = (bf16[16,256,128]{2,1,0:T(8,128)(2,1)S(1)}, bf16[16,256,128]{2,1,0:T(8,128)(2,1)}, u32[]{:S(2)}) copy-start(bf16[16,256,128]{2,1,0:T(8,128)(2,1)} %basis.3) | copy-start | bytes 3145732
  56.6 36.8 %copy-start.13 = (bf16[1,128,128]{2,1,0:T(8,128)(2,1)S(1)}, bf16[1,128,128]{2,1,0:T(8,128)(2,1)}, u32[]{:S(2)}) copy-start(bf16[1,128,128]{2,1,0:T(8,128)(2,1)} %transfer2.3) | copy-start | bytes 98308
  56.6 36.1 %collective-permute-start.3 = (bf16[128,128]{1,0:T(8,128)(2,1)S(1)}, bf16[128,128]{1,0:T(8,128)(2,1)S(1)}, u32[]{:S(2)}, u32[]{:S(2)}) collective-permute-start(bf16[128,128]{1,0:T(8,128)(2,1)S(1)} %slice_bitcast_fusion), channel_id=1, source_target_pairs={{4,0},{6,2},{8,4},{10,6},{12,8},{14,10},{16,12},{18,14},{20,16},{2... | collective-permute-start | bytes 98312 | tf_op jit(solution)/shard_map/ppermute | solution.py:30
  71.8 21.0 %collective-permute-start.2 = (bf16[128,128]{1,0:T(8,128)(2,1)S(1)}, bf16[128,128]{1,0:T(8,128)(2,1)S(1)}, u32[]{:S(2)}, u32[]{:S(2)}) collective-permute-start(bf16[128,128]{1,0:T(8,128)(2,1)S(1)} %slice_bitcast_fusion), channel_id=1, source_target_pairs={{0,4},{2,6},{4,8},{6,10},{8,12},{10,14},{12,16},{14,18},{16,20},{1... | collective-permute-start | bytes 98312 | tf_op jit(solution)/shard_map/ppermute | solution.py:30
  91.8 1.0 copy-start.8
  92.7 0.6 copy-start.15
  93.4 1.0 %copy-start.7 = (bf16[16,128,128]{2,1,0:T(8,128)(2,1)S(1)}, bf16[16,128,128]{2,1,0:T(8,128)(2,1)}, u32[]{:S(2)}) copy-start(bf16[16,128,128]{2,1,0:T(8,128)(2,1)} %transfer3.3) | copy-start | bytes 1572868
  94.4 1.2 %copy-start.9 = (f32[16,128,128]{2,1,0:T(8,128)S(1)}, f32[16,128,128]{2,1,0:T(8,128)}, u32[]{:S(2)}) copy-start(f32[16,128,128]{2,1,0:T(8,128)} %copy-done.8) | copy-start | bytes 3145732
  95.6 0.9 copy-start.14
  96.5 0.8 copy-start.16
  97.3 0.7 copy-start.18

commit v2 on v0

v2 whole, which is shorter than its diff:
```python
import functools

import jax
import jax.numpy as jnp
from jax import lax
from jax.experimental import pallas as pl
from jax.experimental.pallas import tpu as pltpu
from jax.sharding import Mesh, PartitionSpec as P

TOP1 = 16
TOP0 = 4
FAN = TOP1 // TOP0
LEAF = ("y", "x", "z")
EVERY = ("y", "x", "z", "core")
F32 = jnp.float32
BF16 = jnp.bfloat16
MIB = 1024 * 1024
HBM = pl.BlockSpec(memory_space=pltpu.HBM)
ANY = pl.BlockSpec(memory_space=pl.ANY)
VMEM = pl.BlockSpec(memory_space=pltpu.VMEM)
SMEM = pl.BlockSpec(memory_space=pltpu.SMEM)


def dot(a, b):
    return lax.dot_general(a, b, (((1,), (0,)), ((), ())), preferred_element_type=F32)


def dot_t(a, b):
    return lax.dot_general(a, b, (((0,), (0,)), ((), ())), preferred_element_type=F32)


def rows(start, size):
    return pl.ds(pl.multiple_of(start, 128), size)


def node_index():
    return lax.axis_index("y") * lax.axis_size("x") + lax.axis_index("x")


def device_index():
    return node_index() * lax.axis_size("z") + lax.axis_index("z")


def swapped(block):
    return lax.ppermute(block, "core", [(0, 1), (1, 0)])


def in_hbm(*arrays):
    return [pltpu.with_memory_space_constraint(array, pltpu.HBM) for array in arrays]


def exchanged(block, odd):
    count = lax.axis_size(LEAF)
    pairs = [(i, i + 1) for i in range(1 if odd else 0, count - 1, 2)]
    return lax.ppermute(block, LEAF, pairs + [(b, a) for a, b in pairs])


def settings(limit, flops, moved):
    return dict(
        compiler_params=pltpu.CompilerParams(vmem_limit_bytes=limit * MIB),
        cost_estimate=pl.CostEstimate(flops=flops, bytes_accessed=moved, transcendentals=0),
    )


def edges_kernel(charges, first, second, sems):
    half = first.shape[0]
    odd = lax.rem(device_index(), 2)
    copies = [
        pltpu.make_async_copy(charges.at[rows((1 - odd) * half, half)], first, sems.at[0]),
        pltpu.make_async_copy(charges.at[rows(odd * half, half)], second, sems.at[1]),
    ]
    for copy in copies:
        copy.start()
    for copy in copies:
        copy.wait()


def edges(charges):
    half = charges.shape[0] // 2
    shape = jax.ShapeDtypeStruct((half, charges.shape[1]), BF16)
    return pl.pallas_call(
        edges_kernel,
        in_specs=[HBM],
        out_specs=[ANY, ANY],
        out_shape=[shape, shape],
        scratch_shapes=[pltpu.SemaphoreType.DMA((2,))],
        name="edges",
        **settings(8, 0, 2 * MIB),
    )(*in_hbm(charges))


def moments_kernel(
    groups,
    charges,
    basis,
    transfer3,
    transfer2,
    after,
    moment_out,
    moment2_out,
    spread,
    charge_buf,
    basis_buf,
    transfer3_buf,
    transfer2_buf,
    moment_buf,
    in_sems,
    out_sems,
):
    leaves, box, rank = basis.shape
    per = leaves // groups
    loads = []
    for i in range(groups):
        span = pl.ds(i * per * box, per * box)
        part = pl.ds(i * per, per)
        loads.append(
            [
                pltpu.make_async_copy(charges.at[span], charge_buf.at[span], in_sems.at[0, i]),
                pltpu.make_async_copy(basis.at[part], basis_buf.at[part], in_sems.at[1, i]),
                pltpu.make_async_copy(transfer3.at[part], transfer3_buf.at[part], in_sems.at[2, i]),
            ]
        )
    last = pltpu.make_async_copy(transfer2, transfer2_buf, in_sems.at[0, groups])
    for load in loads:
        for copy in load:
            copy.start()
    last.start()
    total = None
    stores = []
    for i in range(groups):
        for copy in loads[i]:
            copy.wait()
        for leaf in range(i * per, (i + 1) * per):
            moment = dot_t(basis_buf[leaf], charge_buf[pl.ds(leaf * box, box)]).astype(BF16)
            moment_buf[pl.ds(leaf * rank, rank)] = moment
            share = dot_t(transfer3_buf[leaf], moment)
            total = share if total is None else total + share
        size = per * rank
        if i == groups - 1:
            moment2 = total.astype(BF16)
            moment_buf[pl.ds(leaves * rank, rank)] = moment2
            moment2_out[...] = moment2
            size = size + rank
        span = pl.ds(i * per * rank, size)
        copy = pltpu.make_async_copy(moment_buf.at[span], moment_out.at[span], out_sems.at[i])
        copy.start()
        stores.append(copy)
    last.wait()
    term = dot_t(transfer2_buf[0], moment2).astype(BF16)
    for i in range(spread.shape[0]):
        spread[i] = term
    for copy in stores:
        copy.wait()


def moments(charges, basis, transfer3, transfer2, after):
    leaves, box, rank = basis.shape
    width = charges.shape[1]
    groups = 4
    return pl.pallas_call(
        functools.partial(moments_kernel, groups),
        in_specs=[HBM] * 5,
        out_specs=[ANY, VMEM, VMEM],
        out_shape=[
            jax.ShapeDtypeStruct(((leaves + 1) * rank, width), BF16),
            jax.ShapeDtypeStruct((rank, width), BF16),
            jax.ShapeDtypeStruct((TOP1, rank, width), BF16),
        ],
        scratch_shapes=[
            pltpu.VMEM((leaves * box, width), BF16),
            pltpu.VMEM((leaves, box, rank), BF16),
            pltpu.VMEM((leaves, rank, rank), BF16),
            pltpu.VMEM((1, rank, rank), BF16),
            pltpu.VMEM(((leaves + 1) * rank, width), BF16),
            pltpu.SemaphoreType.DMA((3, groups + 1)),
            pltpu.SemaphoreType.DMA((groups,)),
        ],
        name="moments",
        **settings(12, 2 * leaves * rank * width * (box + rank), 6 * MIB),
    )(*in_hbm(charges, basis, transfer3, transfer2, after))


def weights_kernel(
    far0,
    basis,
    transfer3,
    transfer1,
    coupling1,
    coupling0,
    joined,
    upper,
    basis_buf,
    transfer3_buf,
    below_buf,
    own_buf,
    coupling1_buf,
    coupling0_buf,
    sems,
):
    leaves, box, rank = basis.shape
    partners = coupling1.shape[1]
    node = node_index()
    root = node // FAN
    copies = [
        pltpu.make_async_copy(transfer1.at[pl.ds(far0[root] * FAN, FAN)], below_buf, sems.at[0]),
        pltpu.make_async_copy(transfer1.at[pl.ds(node, 1)], own_buf, sems.at[1]),
        pltpu.make_async_copy(coupling1.at[pl.ds(node, 1)], coupling1_buf, sems.at[2]),
        pltpu.make_async_copy(coupling0.at[pl.ds(root, 1)], coupling0_buf, sems.at[3]),
        pltpu.make_async_copy(basis, basis_buf, sems.at[4]),
        pltpu.make_async_copy(transfer3, transfer3_buf, sems.at[5]),
    ]
    for copy in copies:
        copy.start()
    for copy in copies[:4]:
        copy.wait()
    through = dot(own_buf[0], coupling0_buf[0]).astype(BF16)
    for i in range(FAN):
        upper[:, i * rank : (i + 1) * rank] = lax.dot_general(
            through, below_buf[i], (((1,), (1,)), ((), ())), preferred_element_type=F32
        ).astype(BF16)
    for f in range(partners):
        upper[:, (FAN + f) * rank : (FAN + f + 1) * rank] = coupling1_buf[0, f]
    for copy in copies[4:]:
        copy.wait()
    for leaf in range(leaves):
        joined[leaf * box : (leaf + 1) * box] = dot(basis_buf[leaf], transfer3_buf[leaf]).astype(BF16)


def weights(far0, basis, transfer3, transfer1, coupling1, coupling0):
    leaves, box, rank = basis.shape
    partners = coupling1.shape[1]
    return pl.pallas_call(
        weights_kernel,
        in_specs=[SMEM] + [HBM] * 5,
        out_specs=[VMEM, VMEM],
        out_shape=[
            jax.ShapeDtypeStruct((leaves * box, rank), BF16),
            jax.ShapeDtypeStruct((rank, (FAN + partners) * rank), BF16),
        ],
        scratch_shapes=[
            pltpu.VMEM((leaves, box, rank), BF16),
            pltpu.VMEM((leaves, rank, rank), BF16),
            pltpu.VMEM((FAN, rank, rank), BF16),
            pltpu.VMEM((1, rank, rank), BF16),
            pltpu.VMEM((1, partners, rank, rank), BF16),
            pltpu.VMEM((1, rank, rank), BF16),
            pltpu.SemaphoreType.DMA((6,)),
        ],
        name="weights",
        **settings(8, 2 * leaves * box * rank * rank, 3 * MIB),
    )(far0, *in_hbm(basis, transfer3, transfer1, coupling1, coupling0))


def upper_kernel(far1, far0, terms, left, spread):
    node = node_index()
    partners = far1.shape[1]
    source = far0[node // FAN]
    right = jnp.concatenate(
        [terms[source * FAN + i] for i in range(FAN)] + [terms[far1[node, f]] for f in range(partners)],
        axis=0,
    )
    total = dot(left[...], right).astype(BF16)
    for i in range(spread.shape[0]):
        spread[i] = total


def upper(far1, far0, terms, left):
    rank, width = terms.shape[1:]
    fellows = lax.axis_size("z")
    return pl.pallas_call(
        upper_kernel,
        in_specs=[SMEM, SMEM, VMEM, VMEM],
        out_specs=VMEM,
        out_shape=jax.ShapeDtypeStruct((fellows, rank, width), BF16),
        name="upper",
        **settings(8, 2 * left.shape[1] * rank * width, MIB),
    )(far1, far0, terms, left)


def near_kernel(
    near_list,
    first_edge,
    own,
    second_edge,
    mine,
    theirs,
    partial,
    charge_buf,
    mine_buf,
    theirs_buf,
    source_sems,
    sems,
):
    leaves, blocks, box, _ = mine.shape
    edge = first_edge.shape[0]
    device = device_index()
    odd = lax.rem(device, 2)
    first = device * leaves
    core = lax.axis_index("core")
    far_end = edge + leaves * box
    sources = [
        (first_edge, charge_buf.at[rows((1 - odd) * far_end, edge)]),
        (own, charge_buf.at[pl.ds(edge, leaves * box)]),
        (second_edge, charge_buf.at[rows(odd * far_end, edge)]),
    ]
    sources = [
        pltpu.make_async_copy(a, b, source_sems.at[i]) for i, (a, b) in enumerate(sources)
    ]

    def loads(leaf):
        return [
            pltpu.make_async_copy(mine.at[leaf], mine_buf.at[leaf], sems.at[0, leaf]),
            pltpu.make_async_copy(theirs.at[leaf], theirs_buf.at[leaf], sems.at[1, leaf]),
        ]

    def begin(leaf, carry):
        for copy in loads(leaf):
            copy.start()
        return carry

    for copy in sources:
        copy.start()
    lax.fori_loop(0, leaves, begin, 0)
    for copy in sources:
        copy.wait()

    def work(leaf, carry):
        for copy in loads(leaf):
            copy.wait()
        places = [near_list[leaf, core * blocks + s] for s in range(blocks)] + [
            near_list[leaf, (1 - core) * blocks + s] for s in range(blocks)
        ]
        left = jnp.concatenate(
            [mine_buf[leaf, s] for s in range(blocks)] + [theirs_buf[leaf, s] for s in range(blocks)],
            axis=1,
        )
        right = jnp.concatenate(
            [charge_buf[rows((place - first) * box + edge, box)] for place in places], axis=0
        )
        partial[rows(leaf * box, box)] = dot(left, right).astype(BF16)
        return carry

    lax.fori_loop(0, leaves, work, 0)


def near_parts(near_list, first_edge, own, second_edge, mine, theirs):
    leaves, blocks, box, _ = mine.shape
    width = own.shape[1]
    return pl.pallas_call(
        near_kernel,
        in_specs=[SMEM] + [HBM] * 5,
        out_specs=VMEM,
        out_shape=jax.ShapeDtypeStruct((leaves * box, width), BF16),
        scratch_shapes=[
            pltpu.VMEM((2 * leaves * box, width), BF16),
            pltpu.VMEM(mine.shape, BF16),
            pltpu.VMEM(mine.shape, BF16),
            pltpu.SemaphoreType.DMA((3,)),
            pltpu.SemaphoreType.DMA((2, leaves)),
        ],
        name="near_parts",
        **settings(24, 2 * leaves * width * 2 * blocks * box * box, 16 * MIB),
    )(near_list, *in_hbm(first_edge, own, second_edge, mine, theirs))


def far_kernel(
    far_list,
    far2,
    first_message,
    message,
    second_message,
    beside,
    across,
    coupling,
    basis,
    coupling2,
    partial,
    result,
    result2,
    moment_buf,
    moment2_buf,
    coupling_buf,
    basis_buf,
    coupling2_buf,
    source_sems,
    sems,
    other_sems,
):
    leaves, partners, rank, _ = coupling.shape
    box = basis.shape[1]
    tall = leaves * rank
    device = device_index()
    odd = lax.rem(device, 2)
    first = device * leaves
    core = lax.axis_index("core")
    sources = [
        (first_message.at[pl.ds(0, tall)], moment_buf.at[rows((1 - odd) * (2 * tall), tall)]),
        (message.at[pl.ds(0, tall)], moment_buf.at[pl.ds(tall, tall)]),
        (second_message.at[pl.ds(0, tall)], moment_buf.at[rows(odd * (2 * tall), tall)]),
    ]
    sources = [
        pltpu.make_async_copy(a, b, source_sems.at[i]) for i, (a, b) in enumerate(sources)
    ]
    others = [
        (basis, basis_buf),
        (coupling2, coupling2_buf),
        (
            first_message.at[pl.ds(tall, rank)],
            moment2_buf.at[rows((1 + 2 * (1 - odd)) * rank, rank)],
        ),
        (second_message.at[pl.ds(tall, rank)], moment2_buf.at[rows((1 + 2 * odd) * rank, rank)]),
        (beside.at[pl.ds(0, rank)], moment2_buf.at[rows(core * (4 * rank), rank)]),
        (across, moment2_buf.at[rows((1 - core) * (4 * rank), rank)]),
    ]
    others = [pltpu.make_async_copy(a, b, other_sems.at[i]) for i, (a, b) in enumerate(others)]

    def load(leaf):
        return pltpu.make_async_copy(coupling.at[leaf], coupling_buf.at[leaf], sems.at[leaf])

    def begin(leaf, carry):
        load(leaf).start()
        return carry

    for copy in sources:
        copy.start()
    lax.fori_loop(0, leaves, begin, 0)
    for copy in others:
        copy.start()
    for copy in sources:
        copy.wait()
    others[0].wait()

    def work(leaf, carry):
        load(leaf).wait()
        left = jnp.concatenate([coupling_buf[leaf, f] for f in range(partners)], axis=1)
        right = jnp.concatenate(
            [
                moment_buf[rows((far_list[leaf, f] - first + leaves) * rank, rank)]
                for f in range(partners)
            ],
            axis=0,
        )
        far = dot(left, right).astype(BF16)
        span = rows(leaf * box, box)
        result[span] = (partial[span].astype(F32) + dot(basis_buf[leaf], far)).astype(BF16)
        return carry

    lax.fori_loop(0, leaves, work, 0)
    for copy in others[1:]:
        copy.wait()
    total = None
    for f in range(far2.shape[1]):
        share = dot(
            coupling2_buf[0, f], moment2_buf[rows((far2[0, f] - device + 2) * rank, rank)]
        )
        total = share if total is None else total + share
    result2[...] = total


def far_parts(
    far_list, far2, first_message, message, second_message, beside, across, coupling, basis, coupling2, partial
):
    leaves, partners, rank, _ = coupling.shape
    box, width = basis.shape[1], partial.shape[1]
    return pl.pallas_call(
        far_kernel,
        in_specs=[SMEM] * 2 + [HBM] * 3 + [ANY] * 2 + [HBM] * 3 + [VMEM],
        out_specs=[VMEM, VMEM],
        out_shape=[
            jax.ShapeDtypeStruct((leaves * box, width), BF16),
            jax.ShapeDtypeStruct((rank, width), F32),
        ],
        scratch_shapes=[
            pltpu.VMEM((3 * leaves * rank, width), BF16),
            pltpu.VMEM((5 * rank, width), BF16),
            pltpu.VMEM(coupling.shape, BF16),
            pltpu.VMEM(basis.shape, BF16),
            pltpu.VMEM(coupling2.shape, BF16),
            pltpu.SemaphoreType.DMA((3,)),
            pltpu.SemaphoreType.DMA((leaves,)),
            pltpu.SemaphoreType.DMA((6,)),
        ],
        name="far_parts",
        **settings(16, 2 * leaves * width * (partners * rank * rank + box * rank), 8 * MIB),
    )(
        far_list,
        far2,
        *in_hbm(first_message, message, second_message),
        beside,
        across,
        *in_hbm(coupling, basis, coupling2),
        partial,
    )


def finish_kernel(
    groups,
    pieces,
    partial2,
    transfer2,
    partial,
    joined,
    potential,
    transfer2_buf,
    partial_buf,
    joined_buf,
    result_buf,
    sems,
    out_sems,
):
    size = partial.shape[0] // groups
    first = pltpu.make_async_copy(transfer2, transfer2_buf, sems.at[0, groups])
    first.start()
    loads = []
    for i in range(groups):
        span = pl.ds(i * size, size)
        loads.append(
            [
                pltpu.make_async_copy(partial.at[span], partial_buf.at[span], sems.at[0, i]),
                pltpu.make_async_copy(joined.at[span], joined_buf.at[span], sems.at[1, i]),
            ]
        )
    for load in loads:
        for copy in load:
            copy.start()
    total = pieces[0].astype(F32)
    for i in range(1, pieces.shape[0]):
        total = total + pieces[i].astype(F32)
    first.wait()
    local2 = (partial2[...] + dot(transfer2_buf[0], total.astype(BF16))).astype(BF16)
    stores = []
    for i in range(groups):
        for copy in loads[i]:
            copy.wait()
        span = pl.ds(i * size, size)
        result_buf[span] = (partial_buf[span].astype(F32) + dot(joined_buf[span], local2)).astype(BF16)
        copy = pltpu.make_async_copy(result_buf.at[span], potential.at[span], out_sems.at[i])
        copy.start()
        stores.append(copy)
    for copy in stores:
        copy.wait()


def finish(pieces, partial2, transfer2, partial, joined):
    groups = 4
    return pl.pallas_call(
        functools.partial(finish_kernel, groups),
        in_specs=[VMEM, VMEM, HBM, ANY, ANY],
        out_specs=HBM,
        out_shape=jax.ShapeDtypeStruct(partial.shape, BF16),
        scratch_shapes=[
            pltpu.VMEM(transfer2.shape, BF16),
            pltpu.VMEM(partial.shape, BF16),
            pltpu.VMEM(joined.shape, BF16),
            pltpu.VMEM(partial.shape, BF16),
            pltpu.SemaphoreType.DMA((2, groups + 1)),
            pltpu.SemaphoreType.DMA((groups,)),
        ],
        name="finish",
        **settings(12, 2 * partial.shape[0] * partial.shape[1] * joined.shape[1], 4 * MIB),
    )(pieces, partial2, *in_hbm(transfer2), partial, joined)


def two_away(moment2):
    count = lax.axis_size(LEAF)
    both = jnp.concatenate([moment2, swapped(moment2)], axis=0)
    route = [(2 * i, 2 * (i + 2)) for i in range(count - 2)]
    route += [(2 * i + 1, 2 * (i - 2) + 1) for i in range(2, count)]
    beside = lax.ppermute(both, EVERY, route)
    return beside, swapped(beside[moment2.shape[0] :])


def body(
    charges,
    leaf_basis,
    transfer3,
    transfer2,
    transfer1,
    coupling3,
    coupling2,
    coupling1,
    coupling0,
    near_blocks,
    near_list,
    far_list3,
    far_list2,
    far_list1,
    far_list0,
):
    leaves, box, width = charges.shape
    other_blocks = swapped(near_blocks)
    flat = charges.reshape(leaves * box, width)
    edge_one, edge_two = edges(flat)
    first_edge = exchanged(edge_one, False)
    second_edge = exchanged(edge_two, True)
    message, moment2, spread = moments(flat, leaf_basis, transfer3, transfer2, edge_one)
    terms = lax.all_to_all(spread, ("y", "x"), 0, 0, tiled=True)
    first_message = exchanged(message, False)
    second_message = exchanged(message, True)
    beside, across = two_away(moment2)
    joined, left = weights(far_list0, leaf_basis, transfer3, transfer1, coupling1, coupling0)
    pieces = upper(far_list1, far_list0, terms, left)
    pieces = lax.all_to_all(pieces, "z", 0, 0, tiled=True)
    partial = near_parts(near_list, first_edge, flat, second_edge, near_blocks, other_blocks)
    partial, partial2 = far_parts(
        far_list3,
        far_list2,
        first_message,
        message,
        second_message,
        beside,
        across,
        coupling3,
        leaf_basis,
        coupling2,
        partial,
    )
    potential = finish(pieces, partial2, transfer2, partial, joined)
    return potential.reshape(leaves, box, width)


def solution(mesh):
    grid = Mesh(mesh.devices.reshape(4, 4, 8, 2), ("y", "x", "z", "core"))
    placed = (
        P(LEAF, None, "core"),
        P(LEAF, None, None),
        P(LEAF, None, None),
        P(LEAF, None, None),
        P(),
        P(LEAF, None, None, None),
        P(LEAF, None, None, None),
        P(),
        P(),
        P(LEAF, "core", None, None),
        P(LEAF, None),
        P(LEAF, None),
        P(LEAF, None),
        P(),
        P(),
    )
    return jax.shard_map(
        body, mesh=grid, in_specs=placed, out_specs=P(LEAF, None, "core"), check_vma=False
    )
```

time: 801 us -> 75.3 us (0.09)
  the two profiles are of different devices: /device:TPU:32 before, /device:TPU:7 now
where the time goes in v2:
time: 75.3 us; the launch traced here: 74.8 us
  Pallas kernels  31.4 us (42%)
  starting transfers between devices  31 us (41%)
  waiting for transfers between devices  9.83 us (13%)
  local copies, waits for them, and re-layouts  2.37 us (3%)
    ppermute x4, starting transfers between devices, exchanged(): return lax.ppermute(block, LEAF, pairs + [(b, a) for a, b in pairs])  10.5 us
    pallas_call x1, Pallas kernels, far_parts(): pl.pallas_call(far_kernel, in_specs=[SMEM] * 2 + [HBM] * 3 + [ANY] * 2 +...  10.4 us
    ppermute x1, waiting for transfers between devices, two_away(): beside = lax.ppermute(both, EVERY, route)  9.81 us
    all_to_all x1, starting transfers between devices, body(): pieces = lax.all_to_all(pieces, 'z', 0, 0, tiled=True)  9.18 us
    pallas_call x1, Pallas kernels, near_parts(): pl.pallas_call(near_kernel, in_specs=[SMEM] + [HBM] * 5, out_specs=VMEM,...  8.54 us
    all_to_all x1, starting transfers between devices, body(): terms = lax.all_to_all(spread, ('y', 'x'), 0, 0, tiled=True)  6.87 us
    pallas_call x1, Pallas kernels, moments(): pl.pallas_call(functools.partial(moments_kernel, groups), in_specs=[HBM]...  4.26 us
    ppermute x1, starting transfers between devices, two_away(): beside = lax.ppermute(both, EVERY, route)  3.08 us
  transfers between devices with their start and end apart: 10, of which 1 were waited for; matrix products, arithmetic and copies ran while one was open for 1% of the time, Pallas kernels for 38%

profile of v2, /device:TPU:7, one launch (start us, length us, event | category | flops | bytes accessed | tf_op | source)
XLA Modules:
  0.0 74.8 jit_solution(16197514871950933777)
XLA Ops:
  0.0 0.7 collective-permute-start.7
  0.7 1.2 %edges.1 = (bf16[2048,128]{1,0:T(8,128)(2,1)S(1)}, bf16[2048,128]{1,0:T(8,128)(2,1)S(1)}) custom-call(bf16[4096,128]{1,0:T(8,128)(2,1)} %bitcast.2), custom_call_target="tpu_custom_call" | custom-call | bytes 2097152 | tf_op jit(solution)/shard_map/edges/pallas_call | solution.py:81
  1.9 0.8 %copy-done.1 = bf16[2048,128]{1,0:T(8,128)(2,1)} copy-done((bf16[2048,128]{1,0:T(8,128)(2,1)}, bf16[2048,128]{1,0:T(8,128)(2,1)S(1)}, u32[]{:S(2)}) %copy-start.1) | copy-done | bytes 524312
  2.7 4.3 %moments.1 = (bf16[2176,128]{1,0:T(8,128)(2,1)S(1)}, bf16[128,128]{1,0:T(8,128)(2,1)S(1)}, bf16[16,128,128]{2,1,0:T(8,128)(2,1)}) custom-call(bf16[4096,128]{1,0:T(8,128)(2,1)} %bitcast.3, bf16[16,256,128]{2,1,0:T(8,128)(2,1)} %basis.5, bf16[16,128,128]{2,1,0:T(8,128)(2,1)} %transfer3.3, bf16[1,128,128]{2,1,0:T(8,128)(2,1)} %transfer2.3, ...), custom_call_target="tpu_custom_call" | custom-call | flops 201326592 | bytes 6291456 | tf_op jit(solution)/shard_map/moments/pallas_call | solution.py:160
  7.0 0.0 copy-start
  7.0 6.9 %all-to-all-start = ((bf16[16,128,128]{2,1,0:T(8,128)(2,1)}), bf16[16,128,128]{2,1,0:T(8,128)(2,1)S(1)}, u32[]{:S(2)}, u32[]{:S(2)}) async-start(bf16[16,128,128]{2,1,0:T(8,128)(2,1)} %get-tuple-element.15), calls=%async_computation | async-start | bytes 1048576 | tf_op jit(solution)/shard_map/all_to_all | solution.py:597
  13.8 0.6 collective-permute-start.2
  14.4 1.7 %collective-permute-start.5 = (bf16[2048,128]{1,0:T(8,128)(2,1)}, bf16[2048,128]{1,0:T(8,128)(2,1)}, u32[]{:S(2)}, u32[]{:S(2)}) collective-permute-start(bf16[2048,128]{1,0:T(8,128)(2,1)} %copy-done.1), channel_id=1, source_target_pairs={{0,2},{4,6},{8,10},{12,14},{16,18},{20,22},{24,26},{28,30},{32,34}... | collective-permute-start | bytes 1572872 | tf_op jit(solution)/shard_map/ppermute | solution.py:55
  16.1 6.9 %collective-permute-start.6 = (bf16[2048,128]{1,0:T(8,128)(2,1)S(1)}, bf16[2048,128]{1,0:T(8,128)(2,1)}, u32[]{:S(2)}, u32[]{:S(2)}) collective-permute-start(bf16[2048,128]{1,0:T(8,128)(2,1)S(1)} %get-tuple-element.19), channel_id=1, source_target_pairs={{2,4},{6,8},{10,12},{14,16},{18,20},{22,24},{26,28},{30,32},{34,36... | collective-permute-start | bytes 1572872 | tf_op jit(solution)/shard_map/ppermute | solution.py:55
  23.0 0.0 collective-permute-done.2
  23.0 3.1 %collective-permute-start.3 = (bf16[256,128]{1,0:T(8,128)(2,1)S(1)}, bf16[256,128]{1,0:T(8,128)(2,1)S(1)}, u32[]{:S(2)}, u32[]{:S(2)}) collective-permute-start(bf16[256,128]{1,0:T(8,128)(2,1)S(1)} %pad_maximum_fusion), channel_id=1, source_target_pairs={{0,4},{2,6},{4,8},{6,10},{8,12},{10,14},{12,16},{14,18},{16,20},{1... | collective-permute-start | bytes 196616 | tf_op jit(solution)/shard_map/ppermute | solution.py:569
  26.1 0.1 collective-permute-start
  26.2 9.8 %collective-permute-done.3.beside = bf16[256,128]{1,0:T(8,128)(2,1)S(1)} collective-permute-done((bf16[256,128]{1,0:T(8,128)(2,1)S(1)}, bf16[256,128]{1,0:T(8,128)(2,1)S(1)}, u32[]{:S(2)}, u32[]{:S(2)}) %collective-permute-start.3) | collective-permute-done | bytes 65568 | tf_op jit(solution)/shard_map/ppermute | solution.py:569
  36.0 1.9 %collective-permute-start.1 = (bf16[2176,128]{1,0:T(8,128)(2,1)S(1)}, bf16[2176,128]{1,0:T(8,128)(2,1)}, u32[]{:S(2)}, u32[]{:S(2)}) collective-permute-start(bf16[2176,128]{1,0:T(8,128)(2,1)S(1)} %get-tuple-element.17.message), channel_id=1, source_target_pairs={{2,4},{6,8},{10,12},{14,16},{18,20},{22,24},{26,28},{30,32},{34,36... | collective-permute-start | bytes 1671176 | tf_op jit(solution)/shard_map/ppermute | solution.py:55
  37.9 0.8 %copy.16.far1 = s32[16,4]{1,0:T(8,128)S(1)} copy(s32[16,4]{0,1:T(4,128)} %param.28) | data formatting | bytes 512 | tf_op args[13]
  38.7 0.7 copy-done.2
  39.3 2.6 %weights.1 = (bf16[4096,128]{1,0:T(8,128)(2,1)S(1)}, bf16[128,1024]{1,0:T(8,128)(2,1)S(1)}) custom-call(s32[4]{0:T(128)S(1)} %copy-done.2, bf16[16,256,128]{2,1,0:T(8,128)(2,1)} %basis.5, bf16[16,128,128]{2,1,0:T(8,128)(2,1)} %transfer3.3, bf16[16,128,128]{2,1,0:T(8,128)(2,1)} %transfer1.1, bf16[16,4,128,128]{3,2,1,0:T(8,128)(2,1)} %coupling1.1, ...), custom_call_target="tpu_custom_call" | custom-call | flops 134217728 | bytes 3145728 | tf_op jit(solution)/shard_map/weights/pallas_call | solution.py:232
  41.9 0.0 all-to-all-done.terms
  41.9 1.6 %upper.1 = bf16[8,128,128]{2,1,0:T(8,128)(2,1)} custom-call(s32[16,4]{1,0:T(8,128)S(1)} %copy.16.far1, s32[4]{0:T(128)S(1)} %copy-done.2, bf16[16,128,128]{2,1,0:T(8,128)(2,1)S(1)} %all-to-all-done.terms, bf16[128,1024]{1,0:T(8,128)(2,1)S(1)} %get-tuple-element.16.left), custom_call_target="tpu_custom_call" | custom-call | flops 33554432 | bytes 1048576 | tf_op jit(solution)/shard_map/upper/pallas_call | solution.py:270
  43.5 9.2 %all-to-all-start.1 = ((bf16[8,128,128]{2,1,0:T(8,128)(2,1)}), bf16[8,128,128]{2,1,0:T(8,128)(2,1)S(1)}, u32[]{:S(2)}, u32[]{:S(2)}) async-start(bf16[8,128,128]{2,1,0:T(8,128)(2,1)} %upper.1), calls=%async_computation.1 | async-start | bytes 524288 | tf_op jit(solution)/shard_map/all_to_all | solution.py:603
  52.7 0.1 copy.17.near_list
  52.8 0.1 copy.18.far_list
  52.9 0.0 collective-permute-done.5.first_edge
  52.9 0.1 collective-permute-start.4
  53.0 0.0 collective-permute-done.6.second_edge
  53.0 0.0 collective-permute-done.7.theirs
  53.0 8.5 %near_parts.1.partial = bf16[4096,128]{1,0:T(8,128)(2,1)S(1)} custom-call(s32[16,6]{1,0:T(8,128)S(1)} %copy.17.near_list, bf16[2048,128]{1,0:T(8,128)(2,1)} %collective-permute-done.5.first_edge, bf16[4096,128]{1,0:T(8,128)(2,1)} %bitcast.4, bf16[2048,128]{1,0:T(8,128)(2,1)} %collective-permute-done.6.second_edge, bf16[16,3,256,256]{3,2,1,0:T(8,128)(2,1)} %mine.1, ...), custom_call_target="tpu_custom_call" | custom-call | flops 1610612736 | bytes 16777216 | tf_op jit(solution)/shard_map/near_parts/pallas_call | solution.py:349
  61.6 0.0 collective-permute-done.4.across
  61.6 0.0 collective-permute-done.first_message
  61.6 0.0 collective-permute-done.1.second_message
  61.6 10.4 %far_parts.1 = (bf16[4096,128]{1,0:T(8,128)(2,1)S(1)}, f32[128,128]{1,0:T(8,128)S(1)}) custom-call(s32[16,8]{1,0:T(8,128)S(1)} %copy.18.far_list, s32[1,4]{1,0:T(1,128)S(1)} %copy-done.3, bf16[2176,128]{1,0:T(8,128)(2,1)} %collective-permute-done.first_message, bf16[2176,128]{1,0:T(8,128)(2,1)} %copy-done, ...), custom_call_target="tpu_custom_call" | custom-call | flops 671088640 | bytes 8388608 | tf_op jit(solution)/shard_map/far_parts/pallas_call | solution.py:465
  72.0 2.8 %finish.1 = bf16[4096,128]{1,0:T(8,128)(2,1)} custom-call(bf16[8,128,128]{2,1,0:T(8,128)(2,1)S(1)} %all-to-all-done.1.pieces, f32[128,128]{1,0:T(8,128)S(1)} %get-tuple-element.20.partial2, bf16[1,128,128]{2,1,0:T(8,128)(2,1)} %transfer2.3, bf16[4096,128]{1,0:T(8,128)(2,1)S(1)} %get-tuple-element.21.partial, bf16[4096,128]{1,0:T(8,128)(2,1)S(1)} %get-tuple-element.22.joined), custom_call_target="tpu_custom_call" | custom-call | flops 134217728 | bytes 4194304 | tf_op jit(solution)/shard_map/finish/pallas_call | solution.py:546
  (12 shorter events, 0.0 us)
Async XLA Ops:
  0.0 52.7 %copy-start.4 = (s32[16,6]{0,1:T(8,128)S(1)}, s32[16,6]{0,1:T(8,128)}, u32[]{:S(2)}) copy-start(s32[16,6]{0,1:T(8,128)} %param.25) | copy-start | bytes 1156
  0.0 52.8 %copy-start.5 = (s32[16,8]{0,1:T(8,128)S(1)}, s32[16,8]{0,1:T(8,128)}, u32[]{:S(2)}) copy-start(s32[16,8]{0,1:T(8,128)} %param.26) | copy-start | bytes 1540
  0.0 53.0 %collective-permute-start.7 = (bf16[16,3,256,256]{3,2,1,0:T(8,128)(2,1)}, bf16[16,3,256,256]{3,2,1,0:T(8,128)(2,1)}, u32[]{:S(2)}, u32[]{:S(2)}) collective-permute-start(bf16[16,3,256,256]{3,2,1,0:T(8,128)(2,1)} %mine.1), channel_id=1, source_target_pairs={{0,1},{1,0},{2,3},{3,2},{4,5},{5,4},{6,7},{7,6},{8,9},{9,8},{10,11... | collective-permute-start | bytes 18874376 | tf_op jit(solution)/shard_map/ppermute | solution.py:45
  1.9 0.8 %copy-start.1 = (bf16[2048,128]{1,0:T(8,128)(2,1)}, bf16[2048,128]{1,0:T(8,128)(2,1)S(1)}, u32[]{:S(2)}) copy-start(bf16[2048,128]{1,0:T(8,128)(2,1)S(1)} %get-tuple-element.14.after) | copy-start | bytes 1572868
  7.0 54.6 %copy-start = (bf16[2176,128]{1,0:T(8,128)(2,1)}, bf16[2176,128]{1,0:T(8,128)(2,1)S(1)}, u32[]{:S(2)}) copy-start(bf16[2176,128]{1,0:T(8,128)(2,1)S(1)} %get-tuple-element.17.message) | copy-start | bytes 1671172
  7.0 34.9 %all-to-all-start = ((bf16[16,128,128]{2,1,0:T(8,128)(2,1)}), bf16[16,128,128]{2,1,0:T(8,128)(2,1)S(1)}, u32[]{:S(2)}, u32[]{:S(2)}) async-start(bf16[16,128,128]{2,1,0:T(8,128)(2,1)} %get-tuple-element.15), calls=%async_computation | async-start | bytes 1048576 | tf_op jit(solution)/shard_map/all_to_all | solution.py:597
  13.8 9.1 %collective-permute-start.2 = (bf16[128,128]{1,0:T(8,128)(2,1)S(1)}, bf16[128,128]{1,0:T(8,128)(2,1)S(1)}, u32[]{:S(2)}, u32[]{:S(2)}) collective-permute-start(bf16[128,128]{1,0:T(8,128)(2,1)S(1)} %get-tuple-element.18), channel_id=1, source_target_pairs={{0,1},{1,0},{2,3},{3,2},{4,5},{5,4},{6,7},{7,6},{8,9},{9,8},{10,11... | collective-permute-start | bytes 98312 | tf_op jit(solution)/shard_map/ppermute | solution.py:45
  14.4 38.4 %collective-permute-start.5 = (bf16[2048,128]{1,0:T(8,128)(2,1)}, bf16[2048,128]{1,0:T(8,128)(2,1)}, u32[]{:S(2)}, u32[]{:S(2)}) collective-permute-start(bf16[2048,128]{1,0:T(8,128)(2,1)} %copy-done.1), channel_id=1, source_target_pairs={{0,2},{4,6},{8,10},{12,14},{16,18},{20,22},{24,26},{28,30},{32,34}... | collective-permute-start | bytes 1572872 | tf_op jit(solution)/shard_map/ppermute | solution.py:55
  16.1 36.9 %collective-permute-start.6 = (bf16[2048,128]{1,0:T(8,128)(2,1)S(1)}, bf16[2048,128]{1,0:T(8,128)(2,1)}, u32[]{:S(2)}, u32[]{:S(2)}) collective-permute-start(bf16[2048,128]{1,0:T(8,128)(2,1)S(1)} %get-tuple-element.19), channel_id=1, source_target_pairs={{2,4},{6,8},{10,12},{14,16},{18,20},{22,24},{26,28},{30,32},{34,36... | collective-permute-start | bytes 1572872 | tf_op jit(solution)/shard_map/ppermute | solution.py:55
  23.0 13.0 %collective-permute-start.3 = (bf16[256,128]{1,0:T(8,128)(2,1)S(1)}, bf16[256,128]{1,0:T(8,128)(2,1)S(1)}, u32[]{:S(2)}, u32[]{:S(2)}) collective-permute-start(bf16[256,128]{1,0:T(8,128)(2,1)S(1)} %pad_maximum_fusion), channel_id=1, source_target_pairs={{0,4},{2,6},{4,8},{6,10},{8,12},{10,14},{12,16},{14,18},{16,20},{1... | collective-permute-start | bytes 196616 | tf_op jit(solution)/shard_map/ppermute | solution.py:569
  26.1 35.5 %collective-permute-start = (bf16[2176,128]{1,0:T(8,128)(2,1)S(1)}, bf16[2176,128]{1,0:T(8,128)(2,1)}, u32[]{:S(2)}, u32[]{:S(2)}) collective-permute-start(bf16[2176,128]{1,0:T(8,128)(2,1)S(1)} %get-tuple-element.17.message), channel_id=1, source_target_pairs={{0,2},{4,6},{8,10},{12,14},{16,18},{20,22},{24,26},{28,30},{32,34}... | collective-permute-start | bytes 1671176 | tf_op jit(solution)/shard_map/ppermute | solution.py:55
  36.0 25.6 %collective-permute-start.1 = (bf16[2176,128]{1,0:T(8,128)(2,1)S(1)}, bf16[2176,128]{1,0:T(8,128)(2,1)}, u32[]{:S(2)}, u32[]{:S(2)}) collective-permute-start(bf16[2176,128]{1,0:T(8,128)(2,1)S(1)} %get-tuple-element.17.message), channel_id=1, source_target_pairs={{2,4},{6,8},{10,12},{14,16},{18,20},{22,24},{26,28},{30,32},{34,36... | collective-permute-start | bytes 1671176 | tf_op jit(solution)/shard_map/ppermute | solution.py:55
  38.7 0.7 copy-start.2
  43.5 28.5 %all-to-all-start.1 = ((bf16[8,128,128]{2,1,0:T(8,128)(2,1)}), bf16[8,128,128]{2,1,0:T(8,128)(2,1)S(1)}, u32[]{:S(2)}, u32[]{:S(2)}) async-start(bf16[8,128,128]{2,1,0:T(8,128)(2,1)} %upper.1), calls=%async_computation.1 | async-start | bytes 524288 | tf_op jit(solution)/shard_map/all_to_all | solution.py:603
  52.9 8.7 %copy-start.3 = (s32[1,4]{1,0:T(1,128)S(1)}, s32[1,4]{1,0:T(1,128)}, u32[]{:S(2)}) copy-start(s32[1,4]{1,0:T(1,128)} %far2.1) | copy-start | bytes 52
  52.9 8.7 %collective-permute-start.4 = (bf16[128,128]{1,0:T(8,128)(2,1)S(1)}, bf16[128,128]{1,0:T(8,128)(2,1)S(1)}, u32[]{:S(2)}, u32[]{:S(2)}) collective-permute-start(bf16[128,128]{1,0:T(8,128)(2,1)S(1)} %slice.4), channel_id=1, source_target_pairs={{0,1},{1,0},{2,3},{3,2},{4,5},{5,4},{6,7},{7,6},{8,9},{9,8},{10,11... | collective-permute-start | bytes 98312 | tf_op jit(solution)/shard_map/ppermute | solution.py:45

commit v3 on v2

v3 whole, which is shorter than its diff:
```python
import functools

import jax
import jax.numpy as jnp
from jax import lax
from jax.experimental import pallas as pl
from jax.experimental.pallas import tpu as pltpu
from jax.sharding import Mesh, PartitionSpec as P

TOP1 = 16
TOP0 = 4
FAN = TOP1 // TOP0
LEAF = ("y", "x", "z")
F32 = jnp.float32
BF16 = jnp.bfloat16
MIB = 1024 * 1024
NEAR_WORK = 1
FAR_WORK = 20
UPPER_WORK = 1
MOMENTS_WORK = 1
HBM = pl.BlockSpec(memory_space=pltpu.HBM)
ANY = pl.BlockSpec(memory_space=pl.ANY)
VMEM = pl.BlockSpec(memory_space=pltpu.VMEM)
SMEM = pl.BlockSpec(memory_space=pltpu.SMEM)


def dot(a, b):
    return lax.dot_general(a, b, (((1,), (0,)), ((), ())), preferred_element_type=F32)


def dot_t(a, b):
    return lax.dot_general(a, b, (((0,), (0,)), ((), ())), preferred_element_type=F32)


def rows(start, size):
    return pl.ds(pl.multiple_of(start, 128), size)


def node_index():
    return lax.axis_index("y") * lax.axis_size("x") + lax.axis_index("x")


def device_index():
    return node_index() * lax.axis_size("z") + lax.axis_index("z")


def swapped(block):
    return lax.ppermute(block, "core", [(0, 1), (1, 0)])


def in_hbm(*arrays):
    return [pltpu.with_memory_space_constraint(array, pltpu.HBM) for array in arrays]


def exchanged(block, odd):
    count = lax.axis_size(LEAF)
    pairs = [(i, i + 1) for i in range(1 if odd else 0, count - 1, 2)]
    return lax.ppermute(block, LEAF, pairs + [(b, a) for a, b in pairs])


def settings(limit, work=1):
    return dict(
        compiler_params=pltpu.CompilerParams(vmem_limit_bytes=limit * MIB),
        cost_estimate=pl.CostEstimate(flops=work * 10**9, bytes_accessed=1000, transcendentals=0),
    )


def streamed(count, depth, copies, work):
    def begin(i):
        for copy in copies(i):
            copy.start()

    def step(i, carry):
        for copy in copies(i):
            copy.wait()
        pl.when(i + depth < count)(lambda: begin(i + depth))
        work(i)
        return carry

    def first(i, carry):
        begin(i)
        return carry

    lax.fori_loop(0, min(depth, count), first, 0)
    return lambda: lax.fori_loop(0, count, step, 0)


def edges_kernel(charges, first, second, sems):
    half = first.shape[0]
    odd = lax.rem(device_index(), 2)
    copies = [
        pltpu.make_async_copy(charges.at[rows((1 - odd) * half, half)], first, sems.at[0]),
        pltpu.make_async_copy(charges.at[rows(odd * half, half)], second, sems.at[1]),
    ]
    for copy in copies:
        copy.start()
    for copy in copies:
        copy.wait()


def edges(charges):
    half = charges.shape[0] // 2
    shape = jax.ShapeDtypeStruct((half, charges.shape[1]), BF16)
    return pl.pallas_call(
        edges_kernel,
        in_specs=[HBM],
        out_specs=[ANY, ANY],
        out_shape=[shape, shape],
        scratch_shapes=[pltpu.SemaphoreType.DMA((2,))],
        name="edges",
        **settings(8),
    )(*in_hbm(charges))


def moments_kernel(
    groups,
    charges,
    basis,
    transfer3,
    transfer2,
    transfer1,
    coupling1,
    coupling0,
    after,
    moment_out,
    moment2_out,
    spread,
    below,
    own_coupling1,
    own_coupling0,
    charge_buf,
    basis_buf,
    transfer3_buf,
    transfer2_buf,
    moment_buf,
    in_sems,
    out_sems,
    upper_sems,
):
    leaves, box, rank = basis.shape
    per = leaves // groups
    node = node_index()
    root = node // FAN
    loads = []
    for i in range(groups):
        span = pl.ds(i * per * box, per * box)
        part = pl.ds(i * per, per)
        loads.append(
            [
                pltpu.make_async_copy(charges.at[span], charge_buf.at[span], in_sems.at[0, i]),
                pltpu.make_async_copy(basis.at[part], basis_buf.at[part], in_sems.at[1, i]),
            ]
        )
    extra = [
        (transfer3, transfer3_buf),
        (transfer2, transfer2_buf),
        (transfer1, below),
        (coupling1.at[pl.ds(node, 1)], own_coupling1),
        (coupling0.at[pl.ds(root, 1)], own_coupling0),
    ]
    extra = [pltpu.make_async_copy(a, b, upper_sems.at[i]) for i, (a, b) in enumerate(extra)]
    for load in loads:
        for copy in load:
            copy.start()
    for copy in extra:
        copy.start()
    stores = []
    for i in range(groups):
        for copy in loads[i]:
            copy.wait()
        for leaf in range(i * per, (i + 1) * per):
            moment = dot_t(basis_buf[leaf], charge_buf[pl.ds(leaf * box, box)])
            moment_buf[pl.ds(leaf * rank, rank)] = moment.astype(BF16)
        span = pl.ds(i * per * rank, per * rank)
        copy = pltpu.make_async_copy(moment_buf.at[span], moment_out.at[span], out_sems.at[i])
        copy.start()
        stores.append(copy)
    for copy in extra[:2]:
        copy.wait()
    moment2 = dot_t(transfer3_buf[...], moment_buf[pl.ds(0, leaves * rank)]).astype(BF16)
    moment_buf[pl.ds(leaves * rank, rank)] = moment2
    span = pl.ds(leaves * rank, rank)
    copy = pltpu.make_async_copy(moment_buf.at[span], moment_out.at[span], out_sems.at[groups])
    copy.start()
    stores.append(copy)
    moment2_out[...] = moment2
    term = dot_t(transfer2_buf[0], moment2).astype(BF16)
    for i in range(spread.shape[0]):
        spread[i] = term
    for copy in stores + extra[2:]:
        copy.wait()


def moments(charges, basis, transfer3, transfer2, transfer1, coupling1, coupling0, after):
    leaves, box, rank = basis.shape
    width = charges.shape[1]
    partners = coupling1.shape[1]
    groups = 4
    return pl.pallas_call(
        functools.partial(moments_kernel, groups),
        in_specs=[HBM] * 7 + [ANY],
        out_specs=[ANY] + [VMEM] * 5,
        out_shape=[
            jax.ShapeDtypeStruct(((leaves + 1) * rank, width), BF16),
            jax.ShapeDtypeStruct((rank, width), BF16),
            jax.ShapeDtypeStruct((TOP1, rank, width), BF16),
            jax.ShapeDtypeStruct(transfer1.shape, BF16),
            jax.ShapeDtypeStruct((1, partners, rank, rank), BF16),
            jax.ShapeDtypeStruct((1, rank, rank), BF16),
        ],
        scratch_shapes=[
            pltpu.VMEM((leaves * box, width), BF16),
            pltpu.VMEM((leaves, box, rank), BF16),
            pltpu.VMEM((leaves * rank, rank), BF16),
            pltpu.VMEM((1, rank, rank), BF16),
            pltpu.VMEM(((leaves + 1) * rank, width), BF16),
            pltpu.SemaphoreType.DMA((2, groups)),
            pltpu.SemaphoreType.DMA((groups + 1,)),
            pltpu.SemaphoreType.DMA((6,)),
        ],
        name="moments",
        **settings(12, MOMENTS_WORK),
    )(*in_hbm(charges, basis, transfer3, transfer2, transfer1, coupling1, coupling0), after)


def upper_kernel(far1, far0, terms, below, own_coupling1, own_coupling0, spread):
    rank = below.shape[1]
    node = node_index()
    partners = far1.shape[1]
    source = far0[node // FAN] * FAN
    top = dot_t(
        jnp.concatenate([below[source + i] for i in range(FAN)], axis=0),
        jnp.concatenate([terms[source + i] for i in range(FAN)], axis=0),
    ).astype(BF16)
    local0 = dot(own_coupling0[0], top).astype(BF16)
    left = [own_coupling1[0, f] for f in range(partners)] + [below[node]]
    right = [terms[far1[node, f]] for f in range(partners)] + [local0]
    total = dot(jnp.concatenate(left, axis=1), jnp.concatenate(right, axis=0)).astype(BF16)
    for i in range(spread.shape[0]):
        spread[i] = total


def upper(far1, far0, terms, below, own_coupling1, own_coupling0):
    rank, width = terms.shape[1:]
    fellows = lax.axis_size("z")
    return pl.pallas_call(
        upper_kernel,
        in_specs=[SMEM, SMEM] + [VMEM] * 4,
        out_specs=VMEM,
        out_shape=jax.ShapeDtypeStruct((fellows, rank, width), BF16),
        name="upper",
        **settings(8, UPPER_WORK),
    )(far1, far0, terms, below, own_coupling1, own_coupling0)


def near_kernel(
    groups,
    near_list,
    first_edge,
    own,
    second_edge,
    mine,
    theirs,
    partial,
    charge_buf,
    mine_buf,
    theirs_buf,
    source_sems,
    sems,
):
    leaves, blocks, box, _ = mine.shape
    per = leaves // groups
    edge = first_edge.shape[0]
    device = device_index()
    odd = lax.rem(device, 2)
    first = device * leaves
    core = lax.axis_index("core")
    far_end = edge + leaves * box
    sources = [
        (first_edge, charge_buf.at[rows((1 - odd) * far_end, edge)]),
        (own, charge_buf.at[pl.ds(edge, leaves * box)]),
        (second_edge, charge_buf.at[rows(odd * far_end, edge)]),
    ]
    sources = [
        pltpu.make_async_copy(a, b, source_sems.at[i]) for i, (a, b) in enumerate(sources)
    ]

    def copies(i):
        part = pl.ds(i * per, per)
        return [
            pltpu.make_async_copy(mine.at[part], mine_buf.at[part], sems.at[0, i]),
            pltpu.make_async_copy(theirs.at[part], theirs_buf.at[part], sems.at[1, i]),
        ]

    def work(i):
        for j in range(per):
            leaf = i * per + j
            places = [near_list[leaf, core * blocks + s] for s in range(blocks)] + [
                near_list[leaf, (1 - core) * blocks + s] for s in range(blocks)
            ]
            left = jnp.concatenate(
                [mine_buf[leaf, s] for s in range(blocks)]
                + [theirs_buf[leaf, s] for s in range(blocks)],
                axis=1,
            )
            right = jnp.concatenate(
                [charge_buf[rows((place - first) * box + edge, box)] for place in places], axis=0
            )
            partial[rows(leaf * box, box)] = dot(left, right).astype(BF16)

    for copy in sources:
        copy.start()
    run = streamed(groups, 3, copies, work)
    for copy in sources:
        copy.wait()
    run()


def near_parts(near_list, first_edge, own, second_edge, mine, theirs):
    leaves, blocks, box, _ = mine.shape
    width = own.shape[1]
    groups = leaves // 4
    return pl.pallas_call(
        functools.partial(near_kernel, groups),
        in_specs=[SMEM] + [HBM] * 5,
        out_specs=VMEM,
        out_shape=jax.ShapeDtypeStruct((leaves * box, width), BF16),
        scratch_shapes=[
            pltpu.VMEM((2 * leaves * box, width), BF16),
            pltpu.VMEM(mine.shape, BF16),
            pltpu.VMEM(mine.shape, BF16),
            pltpu.SemaphoreType.DMA((3,)),
            pltpu.SemaphoreType.DMA((2, groups)),
        ],
        name="near_parts",
        **settings(24, NEAR_WORK),
    )(near_list, *in_hbm(first_edge, own, second_edge, mine, theirs))


def far_kernel(
    groups,
    far_list,
    after,
    first_message,
    message,
    second_message,
    coupling,
    result,
    moment_buf,
    coupling_buf,
    source_sems,
    sems,
):
    leaves, partners, rank, _ = coupling.shape
    per = leaves // groups
    tall = leaves * rank
    device = device_index()
    odd = lax.rem(device, 2)
    first = device * leaves
    sources = [
        (first_message.at[pl.ds(0, tall)], moment_buf.at[rows((1 - odd) * (2 * tall), tall)]),
        (message.at[pl.ds(0, tall)], moment_buf.at[pl.ds(tall, tall)]),
        (second_message.at[pl.ds(0, tall)], moment_buf.at[rows(odd * (2 * tall), tall)]),
    ]
    sources = [
        pltpu.make_async_copy(a, b, source_sems.at[i]) for i, (a, b) in enumerate(sources)
    ]

    def copies(i):
        part = pl.ds(i * per, per)
        return [pltpu.make_async_copy(coupling.at[part], coupling_buf.at[part], sems.at[i])]

    def work(i):
        for j in range(per):
            leaf = i * per + j
            left = jnp.concatenate([coupling_buf[leaf, f] for f in range(partners)], axis=1)
            right = jnp.concatenate(
                [
                    moment_buf[rows((far_list[leaf, f] - first + leaves) * rank, rank)]
                    for f in range(partners)
                ],
                axis=0,
            )
            result[rows(leaf * rank, rank)] = dot(left, right).astype(BF16)

    for copy in sources:
        copy.start()
    run = streamed(groups, 3, copies, work)
    for copy in sources:
        copy.wait()
    run()


def far_parts(far_list, after, first_message, message, second_message, coupling):
    leaves, partners, rank, _ = coupling.shape
    width = message.shape[1]
    groups = leaves // 4
    return pl.pallas_call(
        functools.partial(far_kernel, groups),
        in_specs=[SMEM] + [ANY] * 4 + [HBM],
        out_specs=VMEM,
        out_shape=jax.ShapeDtypeStruct((leaves * rank, width), BF16),
        scratch_shapes=[
            pltpu.VMEM((3 * leaves * rank, width), BF16),
            pltpu.VMEM(coupling.shape, BF16),
            pltpu.SemaphoreType.DMA((3,)),
            pltpu.SemaphoreType.DMA((groups,)),
        ],
        name="far_parts",
        **settings(16, FAR_WORK),
    )(far_list, after, first_message, message, second_message, *in_hbm(coupling))


def finish_kernel(
    groups,
    far2,
    pieces,
    near,
    far,
    first_message,
    second_message,
    first_two,
    second_two,
    coupling2,
    transfer2,
    transfer3,
    basis,
    potential,
    moment2_buf,
    coupling2_buf,
    transfer2_buf,
    transfer3_buf,
    basis_buf,
    result_buf,
    local_buf,
    sems,
    out_sems,
):
    leaves, box, rank = basis.shape
    per = leaves // groups
    fellows = pieces.shape[0]
    partners = far2.shape[1]
    first = [
        pltpu.make_async_copy(coupling2, coupling2_buf, sems.at[0]),
        pltpu.make_async_copy(transfer2, transfer2_buf, sems.at[1]),
    ]
    later = pltpu.make_async_copy(transfer3, transfer3_buf, sems.at[2])
    tall = leaves * rank
    device = device_index()
    odd = lax.rem(device, 2)
    upper_half = lax.rem(device, 4) // 2
    sides = [
        (first_message.at[pl.ds(tall, rank)], 3 - 2 * odd),
        (second_message.at[pl.ds(tall, rank)], 1 + 2 * odd),
        (first_two, 4 - 4 * upper_half),
        (second_two, 4 * upper_half),
    ]
    for i, (source, place) in enumerate(sides):
        target = moment2_buf.at[rows(place * rank, rank)]
        first.append(pltpu.make_async_copy(source, target, sems.at[3 + i]))

    def copies(i):
        part = pl.ds(i * per, per)
        return [pltpu.make_async_copy(basis.at[part], basis_buf.at[part], sems.at[7 + i])]

    def store(i):
        span = rows(i * (per * box), per * box)
        return pltpu.make_async_copy(result_buf.at[span], potential.at[span], out_sems.at[i])

    def work(i):
        for j in range(per):
            leaf = i * per + j
            span = rows(leaf * box, box)
            share = dot(basis_buf[leaf], local_buf[rows(leaf * rank, rank)])
            result_buf[span] = (near[span].astype(F32) + share).astype(BF16)
        store(i).start()

    for copy in first + [later]:
        copy.start()
    run = streamed(groups, groups, copies, work)
    total = pieces[0].astype(F32)
    for i in range(1, fellows):
        total = total + pieces[i].astype(F32)
    for copy in first:
        copy.wait()
    right = [moment2_buf[rows((far2[0, f] - device + 2) * rank, rank)] for f in range(partners)]
    right = jnp.concatenate(right + [total.astype(BF16)], axis=0)
    left = [coupling2_buf[0, f] for f in range(partners)] + [transfer2_buf[0]]
    local2 = dot(jnp.concatenate(left, axis=1), right).astype(BF16)
    later.wait()
    local_buf[...] = (far[...].astype(F32) + dot(transfer3_buf[...], local2)).astype(BF16)
    run()

    def finished(i, carry):
        store(i).wait()
        return carry

    lax.fori_loop(0, groups, finished, 0)


def finish(far2, pieces, near, far, sides, coupling2, transfer2, transfer3, basis):
    leaves, box, rank = basis.shape
    groups = 4
    return pl.pallas_call(
        functools.partial(finish_kernel, groups),
        in_specs=[SMEM] + [VMEM] * 3 + [ANY] * 4 + [HBM] * 4,
        out_specs=HBM,
        out_shape=jax.ShapeDtypeStruct(near.shape, BF16),
        scratch_shapes=[
            pltpu.VMEM((5 * rank, near.shape[1]), BF16),
            pltpu.VMEM(coupling2.shape, BF16),
            pltpu.VMEM(transfer2.shape, BF16),
            pltpu.VMEM(transfer3.shape, BF16),
            pltpu.VMEM(basis.shape, BF16),
            pltpu.VMEM(near.shape, BF16),
            pltpu.VMEM(far.shape, BF16),
            pltpu.SemaphoreType.DMA((7 + groups,)),
            pltpu.SemaphoreType.DMA((groups,)),
        ],
        name="finish",
        **settings(12),
    )(far2, pieces, near, far, *sides, *in_hbm(coupling2, transfer2, transfer3, basis))


def two_away(block, odd):
    count = lax.axis_size(LEAF)
    pairs = [(i, i + 2) for i in range(count - 2) if i // 2 % 2 == odd]
    return lax.ppermute(block, LEAF, pairs + [(b, a) for a, b in pairs])


def body(
    charges,
    leaf_basis,
    transfer3,
    transfer2,
    transfer1,
    coupling3,
    coupling2,
    coupling1,
    coupling0,
    near_blocks,
    near_list,
    far_list3,
    far_list2,
    far_list1,
    far_list0,
):
    leaves, box, width = charges.shape
    rank = leaf_basis.shape[2]
    other_blocks = swapped(near_blocks)
    flat = charges.reshape(leaves * box, width)
    transfer3 = transfer3.reshape(leaves * rank, rank)
    edge_one, edge_two = edges(flat)
    first_edge = exchanged(edge_one, False)
    second_edge = exchanged(edge_two, True)
    message, moment2, spread, *parts = moments(
        flat, leaf_basis, transfer3, transfer2, transfer1, coupling1, coupling0, edge_one
    )
    terms = lax.all_to_all(spread, ("y", "x"), 0, 0, tiled=True)
    first_message = exchanged(message, False)
    first_two = two_away(moment2, 0)
    second_two = two_away(moment2, 1)
    terms, first_edge, second_edge, first_two, second_two, late = lax.optimization_barrier(
        (terms, first_edge, second_edge, first_two, second_two, message)
    )
    second_message = exchanged(late, True)
    pieces = upper(far_list1, far_list0, terms, *parts)
    pieces = lax.all_to_all(pieces, "z", 0, 0, tiled=True)
    near = near_parts(near_list, first_edge, flat, second_edge, near_blocks, other_blocks)
    far = far_parts(far_list3, near, first_message, message, second_message, coupling3)
    sides = first_message, second_message, first_two, second_two
    potential = finish(far_list2, pieces, near, far, sides, coupling2, transfer2, transfer3, leaf_basis)
    return potential.reshape(leaves, box, width)


def solution(mesh):
    grid = Mesh(mesh.devices.reshape(4, 4, 8, 2), ("y", "x", "z", "core"))
    placed = (
        P(LEAF, None, "core"),
        P(LEAF, None, None),
        P(LEAF, None, None),
        P(LEAF, None, None),
        P(),
        P(LEAF, None, None, None),
        P(LEAF, None, None, None),
        P(),
        P(),
        P(LEAF, "core", None, None),
        P(LEAF, None),
        P(LEAF, None),
        P(LEAF, None),
        P(),
        P(),
    )
    return jax.shard_map(
        body, mesh=grid, in_specs=placed, out_specs=P(LEAF, None, "core"), check_vma=False
    )
```

time: 75.3 us -> 65.4 us (0.87)
  the two profiles are of different devices: /device:TPU:7 before, /device:TPU:24 now
where the time goes in v3:
time: 65.4 us; the launch traced here: 65 us
  starting transfers between devices  35 us (54%)
  Pallas kernels  22.2 us (34%)
  waiting for transfers between devices  6.51 us (10%)
  local copies, waits for them, and re-layouts  1.05 us (2%)
    ppermute x4, starting transfers between devices, exchanged(): return lax.ppermute(block, LEAF, pairs + [(b, a) for a, b in pairs])  20.5 us
    pallas_call x1, Pallas kernels, near_parts(): pl.pallas_call(functools.partial(near_kernel, groups), in_specs=[SMEM] +...  7.22 us
    ppermute x2, starting transfers between devices, two_away(): return lax.ppermute(block, LEAF, pairs + [(b, a) for a, b in pairs])  6.21 us
    all_to_all x1, starting transfers between devices, body(): terms = lax.all_to_all(spread, ('y', 'x'), 0, 0, tiled=True)  4.81 us
    pallas_call x1, Pallas kernels, moments(): pl.pallas_call(functools.partial(moments_kernel, groups), in_specs=[HBM]...  4.07 us
    pallas_call x1, Pallas kernels, far_parts(): pl.pallas_call(functools.partial(far_kernel, groups), in_specs=[SMEM] + [...  3.99 us
    ppermute x4, waiting for transfers between devices, exchanged(): return lax.ppermute(block, LEAF, pairs + [(b, a) for a, b in pairs])  3.91 us
    pallas_call x1, Pallas kernels, finish(): pl.pallas_call(functools.partial(finish_kernel, groups), in_specs=[SMEM]...  3.81 us
  transfers between devices with their start and end apart: 9, of which 2 were waited for; matrix products, arithmetic and copies ran while one was open for 0% of the time, Pallas kernels for 28%

profile of v3, /device:TPU:24, one launch (start us, length us, event | category | flops | bytes accessed | tf_op | source)
XLA Modules:
  0.0 65.0 jit_solution(382606448037866612)
XLA Ops:
  0.0 0.0 copy-start.1
  0.0 0.1 collective-permute-start.4
  0.1 1.2 %edges.1 = (bf16[2048,128]{1,0:T(8,128)(2,1)S(1)}, bf16[2048,128]{1,0:T(8,128)(2,1)S(1)}) custom-call(bf16[4096,128]{1,0:T(8,128)(2,1)} %bitcast.3), custom_call_target="tpu_custom_call" | custom-call | flops 1000000000 | bytes 1000 | tf_op jit(solution)/shard_map/edges/pallas_call | solution.py:104
  1.4 2.0 %collective-permute-start = (bf16[2048,128]{1,0:T(8,128)(2,1)S(1)}, bf16[2048,128]{1,0:T(8,128)(2,1)S(1)}, u32[]{:S(2)}, u32[]{:S(2)}) collective-permute-start(bf16[2048,128]{1,0:T(8,128)(2,1)S(1)} %get-tuple-element.19.after), channel_id=1, source_target_pairs={{0,2},{4,6},{8,10},{12,14},{16,18},{20,22},{24,26},{28,30},{32,34}... | collective-permute-start | bytes 1572872 | tf_op jit(solution)/shard_map/ppermute | solution.py:58
  3.4 9.2 %collective-permute-start.1 = (bf16[2048,128]{1,0:T(8,128)(2,1)S(1)}, bf16[2048,128]{1,0:T(8,128)(2,1)}, u32[]{:S(2)}, u32[]{:S(2)}) collective-permute-start(bf16[2048,128]{1,0:T(8,128)(2,1)S(1)} %get-tuple-element.21), channel_id=1, source_target_pairs={{2,4},{6,8},{10,12},{14,16},{18,20},{22,24},{26,28},{30,32},{34,36... | collective-permute-start | bytes 1572872 | tf_op jit(solution)/shard_map/ppermute | solution.py:58
  12.6 4.1 %moments.1 = (bf16[2176,128]{1,0:T(8,128)(2,1)}, bf16[128,128]{1,0:T(8,128)(2,1)S(1)}, bf16[16,128,128]{2,1,0:T(8,128)(2,1)}, bf16[16,128,128]{2,1,0:T(8,128)(2,...) custom-call(bf16[4096,128]{1,0:T(8,128)(2,1)} %bitcast.4, bf16[16,256,128]{2,1,0:T(8,128)(2,1)} %basis.3, ...), custom_call_target="tpu_custom_call" | custom-call | flops 1000000000 | bytes 1000 | tf_op jit(solution)/shard_map/moments/pallas_call | solution.py:199
  16.7 4.8 %all-to-all-start = ((bf16[16,128,128]{2,1,0:T(8,128)(2,1)}), bf16[16,128,128]{2,1,0:T(8,128)(2,1)S(1)}, u32[]{:S(2)}, u32[]{:S(2)}) async-start(bf16[16,128,128]{2,1,0:T(8,128)(2,1)} %get-tuple-element.20), calls=%async_computation | async-start | bytes 1048576 | tf_op jit(solution)/shard_map/all_to_all | solution.py:559
  21.5 0.0 collective-permute-start.2
  21.5 6.2 %collective-permute-start.3 = (bf16[128,128]{1,0:T(8,128)(2,1)S(1)}, bf16[128,128]{1,0:T(8,128)(2,1)S(1)}, u32[]{:S(2)}, u32[]{:S(2)}) collective-permute-start(bf16[128,128]{1,0:T(8,128)(2,1)S(1)} %get-tuple-element.22), channel_id=1, source_target_pairs={{4,8},{6,10},{12,16},{14,18},{20,24},{22,26},{28,32},{30,34},{36,4... | collective-permute-start | bytes 98312 | tf_op jit(solution)/shard_map/ppermute | solution.py:528
  27.7 0.0 collective-permute-done.2.first_two
  27.7 2.1 %collective-permute-start.5 = (bf16[2176,128]{1,0:T(8,128)(2,1)}, bf16[2176,128]{1,0:T(8,128)(2,1)S(1)}, u32[]{:S(2)}, u32[]{:S(2)}) collective-permute-start(bf16[2176,128]{1,0:T(8,128)(2,1)} %get-tuple-element.30.message), channel_id=1, source_target_pairs={{0,2},{4,6},{8,10},{12,14},{16,18},{20,22},{24,26},{28,30},{32,34}... | collective-permute-start | bytes 1671176 | tf_op jit(solution)/shard_map/ppermute | solution.py:58
  29.8 2.6 %collective-permute-done.3.second_two = bf16[128,128]{1,0:T(8,128)(2,1)S(1)} collective-permute-done((bf16[128,128]{1,0:T(8,128)(2,1)S(1)}, bf16[128,128]{1,0:T(8,128)(2,1)S(1)}, u32[]{:S(2)}, u32[]{:S(2)}) %collective-permute-start.3) | collective-permute-done | bytes 32800 | tf_op jit(solution)/shard_map/ppermute | solution.py:528
  32.4 0.0 all-to-all-done.terms
  32.4 0.0 collective-permute-done.first_edge
  32.4 0.8 %copy-done.2 = bf16[2048,128]{1,0:T(8,128)(2,1)} copy-done((bf16[2048,128]{1,0:T(8,128)(2,1)}, bf16[2048,128]{1,0:T(8,128)(2,1)S(1)}, u32[]{:S(2)}) %copy-start.2) | copy-done | bytes 524312
  33.2 0.0 collective-permute-done.1.second_edge
  33.2 7.2 %collective-permute-start.6 = (bf16[2176,128]{1,0:T(8,128)(2,1)}, bf16[2176,128]{1,0:T(8,128)(2,1)S(1)}, u32[]{:S(2)}, u32[]{:S(2)}) collective-permute-start(bf16[2176,128]{1,0:T(8,128)(2,1)} %get-tuple-element.30.message), channel_id=1, source_target_pairs={{2,4},{6,8},{10,12},{14,16},{18,20},{22,24},{26,28},{30,32},{34,36... | collective-permute-start | bytes 1671176 | tf_op jit(solution)/shard_map/ppermute | solution.py:58
  40.4 0.0 copy-done.5
  40.4 0.1 copy.16.far1
  40.5 0.0 copy-done.3
  40.5 0.1 copy.17.near_list
  40.6 0.1 copy.18.far_list
  40.7 1.9 %upper.1 = bf16[8,128,128]{2,1,0:T(8,128)(2,1)} custom-call(s32[16,4]{1,0:T(8,128)S(1)} %copy.16.far1, s32[4]{0:T(128)S(1)} %copy-done.1, bf16[16,128,128]{2,1,0:T(8,128)(2,1)S(1)} %all-to-all-done.terms, bf16[16,128,128]{2,1,0:T(8,128)(2,1)S(1)} %get-tuple-element.25.below, bf16[1,4,128,128]{3,2,1,0:T(8,128)(2,1)S(1)} %get-tuple-element.26.own_coupling1, ...), custom_call_target="tpu_custom_call" | custom-call | flops 1000000000 | bytes 1000 | tf_op jit(solution)/shard_map/upper/pallas_call | solution.py:246
  42.6 3.4 %all-to-all-start.1 = ((bf16[8,128,128]{2,1,0:T(8,128)(2,1)}), bf16[8,128,128]{2,1,0:T(8,128)(2,1)S(1)}, u32[]{:S(2)}, u32[]{:S(2)}) async-start(bf16[8,128,128]{2,1,0:T(8,128)(2,1)} %upper.1), calls=%async_computation.1 | async-start | bytes 524288 | tf_op jit(solution)/shard_map/all_to_all | solution.py:568
  46.0 0.0 collective-permute-done.4.theirs
  46.0 7.2 %near_parts.1.after.near = bf16[4096,128]{1,0:T(8,128)(2,1)S(1)} custom-call(s32[16,6]{1,0:T(8,128)S(1)} %copy.17.near_list, bf16[2048,128]{1,0:T(8,128)(2,1)} %copy-done.2, bf16[4096,128]{1,0:T(8,128)(2,1)} %bitcast.5, bf16[2048,128]{1,0:T(8,128)(2,1)} %collective-permute-done.1.second_edge, bf16[16,3,256,256]{3,2,1,0:T(8,128)(2,1)} %mine.1, ...), custom_call_target="tpu_custom_call" | custom-call | flops 1000000000 | bytes 1000 | tf_op jit(solution)/shard_map/near_parts/pallas_call | solution.py:323
  53.2 0.0 copy-start
  53.2 0.0 collective-permute-done.5.first_message
  53.2 3.9 %collective-permute-done.6.second_message = bf16[2176,128]{1,0:T(8,128)(2,1)S(1)} collective-permute-done((bf16[2176,128]{1,0:T(8,128)(2,1)}, bf16[2176,128]{1,0:T(8,128)(2,1)S(1)}, u32[]{:S(2)}, u32[]{:S(2)}) %collective-permute-start.6) | collective-permute-done | bytes 557088 | tf_op jit(solution)/shard_map/ppermute | solution.py:58
  57.1 4.0 %far_parts.1.far = bf16[2048,128]{1,0:T(8,128)(2,1)S(1)} custom-call(s32[16,8]{1,0:T(8,128)S(1)} %copy.18.far_list, bf16[4096,128]{1,0:T(8,128)(2,1)S(1)} %near_parts.1.after.near, bf16[2176,128]{1,0:T(8,128)(2,1)S(1)} %collective-permute-done.5.first_message, bf16[2176,128]{1,0:T(8,128)(2,1)} %get-tuple-element.30.message, ...), custom_call_target="tpu_custom_call" | custom-call | flops 20000000000 | bytes 1000 | tf_op jit(solution)/shard_map/far_parts/pallas_call | solution.py:398
  61.1 0.0 all-to-all-done.1.pieces
  61.2 3.8 %finish.1 = bf16[4096,128]{1,0:T(8,128)(2,1)} custom-call(s32[1,4]{1,0:T(1,128)S(1)} %copy-done, bf16[8,128,128]{2,1,0:T(8,128)(2,1)S(1)} %all-to-all-done.1.pieces, bf16[4096,128]{1,0:T(8,128)(2,1)S(1)} %near_parts.1.after.near, bf16[2048,128]{1,0:T(8,128)(2,1)S(1)} %far_parts.1.far, bf16[2176,128]{1,0:T(8,128)(2,1)S(1)} %collective-permute-done.5.first_message, ...), custom_call_target="tpu_custom_call" | custom-call | flops 1000000000 | bytes 1000 | tf_op jit(solution)/shard_map/finish/pallas_call | solution.py:504
  (7 shorter events, 0.0 us)
Async XLA Ops:
  0.0 40.4 %copy-start.5 = (s32[16,4]{0,1:T(4,128)S(1)}, s32[16,4]{0,1:T(4,128)}, u32[]{:S(2)}) copy-start(s32[16,4]{0,1:T(4,128)} %param.28) | copy-start | bytes 772
  0.0 40.5 %copy-start.3 = (s32[16,6]{0,1:T(8,128)S(1)}, s32[16,6]{0,1:T(8,128)}, u32[]{:S(2)}) copy-start(s32[16,6]{0,1:T(8,128)} %param.25) | copy-start | bytes 1156
  0.0 40.6 %copy-start.4 = (s32[16,8]{0,1:T(8,128)S(1)}, s32[16,8]{0,1:T(8,128)}, u32[]{:S(2)}) copy-start(s32[16,8]{0,1:T(8,128)} %param.26) | copy-start | bytes 1540
  0.0 40.6 %copy-start.1 = (s32[4]{0:T(128)S(1)}, s32[4]{0:T(128)}, u32[]{:S(2)}) copy-start(s32[4]{0:T(128)} %far0.1) | copy-start | bytes 52
  0.0 46.0 %collective-permute-start.4 = (bf16[16,3,256,256]{3,2,1,0:T(8,128)(2,1)}, bf16[16,3,256,256]{3,2,1,0:T(8,128)(2,1)}, u32[]{:S(2)}, u32[]{:S(2)}) collective-permute-start(bf16[16,3,256,256]{3,2,1,0:T(8,128)(2,1)} %mine.1), channel_id=1, source_target_pairs={{0,1},{1,0},{2,3},{3,2},{4,5},{5,4},{6,7},{7,6},{8,9},{9,8},{10,11... | collective-permute-start | bytes 18874376 | tf_op jit(solution)/shard_map/ppermute | solution.py:48
  1.4 31.1 %collective-permute-start = (bf16[2048,128]{1,0:T(8,128)(2,1)S(1)}, bf16[2048,128]{1,0:T(8,128)(2,1)S(1)}, u32[]{:S(2)}, u32[]{:S(2)}) collective-permute-start(bf16[2048,128]{1,0:T(8,128)(2,1)S(1)} %get-tuple-element.19.after), channel_id=1, source_target_pairs={{0,2},{4,6},{8,10},{12,14},{16,18},{20,22},{24,26},{28,30},{32,34}... | collective-permute-start | bytes 1572872 | tf_op jit(solution)/shard_map/ppermute | solution.py:58
  3.4 29.8 %collective-permute-start.1 = (bf16[2048,128]{1,0:T(8,128)(2,1)S(1)}, bf16[2048,128]{1,0:T(8,128)(2,1)}, u32[]{:S(2)}, u32[]{:S(2)}) collective-permute-start(bf16[2048,128]{1,0:T(8,128)(2,1)S(1)} %get-tuple-element.21), channel_id=1, source_target_pairs={{2,4},{6,8},{10,12},{14,16},{18,20},{22,24},{26,28},{30,32},{34,36... | collective-permute-start | bytes 1572872 | tf_op jit(solution)/shard_map/ppermute | solution.py:58
  16.7 15.7 %all-to-all-start = ((bf16[16,128,128]{2,1,0:T(8,128)(2,1)}), bf16[16,128,128]{2,1,0:T(8,128)(2,1)S(1)}, u32[]{:S(2)}, u32[]{:S(2)}) async-start(bf16[16,128,128]{2,1,0:T(8,128)(2,1)} %get-tuple-element.20), calls=%async_computation | async-start | bytes 1048576 | tf_op jit(solution)/shard_map/all_to_all | solution.py:559
  21.5 6.2 %collective-permute-start.2 = (bf16[128,128]{1,0:T(8,128)(2,1)S(1)}, bf16[128,128]{1,0:T(8,128)(2,1)S(1)}, u32[]{:S(2)}, u32[]{:S(2)}) collective-permute-start(bf16[128,128]{1,0:T(8,128)(2,1)S(1)} %get-tuple-element.22), channel_id=1, source_target_pairs={{0,4},{2,6},{8,12},{10,14},{16,20},{18,22},{24,28},{26,30},{32,36}... | collective-permute-start | bytes 98312 | tf_op jit(solution)/shard_map/ppermute | solution.py:528
  21.5 10.9 %collective-permute-start.3 = (bf16[128,128]{1,0:T(8,128)(2,1)S(1)}, bf16[128,128]{1,0:T(8,128)(2,1)S(1)}, u32[]{:S(2)}, u32[]{:S(2)}) collective-permute-start(bf16[128,128]{1,0:T(8,128)(2,1)S(1)} %get-tuple-element.22), channel_id=1, source_target_pairs={{4,8},{6,10},{12,16},{14,18},{20,24},{22,26},{28,32},{30,34},{36,4... | collective-permute-start | bytes 98312 | tf_op jit(solution)/shard_map/ppermute | solution.py:528
  27.7 25.5 %collective-permute-start.5 = (bf16[2176,128]{1,0:T(8,128)(2,1)}, bf16[2176,128]{1,0:T(8,128)(2,1)S(1)}, u32[]{:S(2)}, u32[]{:S(2)}) collective-permute-start(bf16[2176,128]{1,0:T(8,128)(2,1)} %get-tuple-element.30.message), channel_id=1, source_target_pairs={{0,2},{4,6},{8,10},{12,14},{16,18},{20,22},{24,26},{28,30},{32,34}... | collective-permute-start | bytes 1671176 | tf_op jit(solution)/shard_map/ppermute | solution.py:58
  32.4 0.8 %copy-start.2 = (bf16[2048,128]{1,0:T(8,128)(2,1)}, bf16[2048,128]{1,0:T(8,128)(2,1)S(1)}, u32[]{:S(2)}) copy-start(bf16[2048,128]{1,0:T(8,128)(2,1)S(1)} %collective-permute-done.first_edge) | copy-start | bytes 1572868
  33.2 23.9 %collective-permute-start.6 = (bf16[2176,128]{1,0:T(8,128)(2,1)}, bf16[2176,128]{1,0:T(8,128)(2,1)S(1)}, u32[]{:S(2)}, u32[]{:S(2)}) collective-permute-start(bf16[2176,128]{1,0:T(8,128)(2,1)} %get-tuple-element.30.message), channel_id=1, source_target_pairs={{2,4},{6,8},{10,12},{14,16},{18,20},{22,24},{26,28},{30,32},{34,36... | collective-permute-start | bytes 1671176 | tf_op jit(solution)/shard_map/ppermute | solution.py:58
  42.6 18.6 %all-to-all-start.1 = ((bf16[8,128,128]{2,1,0:T(8,128)(2,1)}), bf16[8,128,128]{2,1,0:T(8,128)(2,1)S(1)}, u32[]{:S(2)}, u32[]{:S(2)}) async-start(bf16[8,128,128]{2,1,0:T(8,128)(2,1)} %upper.1), calls=%async_computation.1 | async-start | bytes 524288 | tf_op jit(solution)/shard_map/all_to_all | solution.py:568
  53.2 7.9 %copy-start = (s32[1,4]{1,0:T(1,128)S(1)}, s32[1,4]{1,0:T(1,128)}, u32[]{:S(2)}) copy-start(s32[1,4]{1,0:T(1,128)} %far2.1) | copy-start | bytes 52

commit v4 on v3

--- a/solution.py
+++ b/solution.py
@@ -14,9 +14,9 @@
 F32 = jnp.float32
 BF16 = jnp.bfloat16
 MIB = 1024 * 1024
-NEAR_WORK = 1
+NEAR_WORK = 5
 FAR_WORK = 20
-UPPER_WORK = 1
+UPPER_WORK = 5
 MOMENTS_WORK = 1
 HBM = pl.BlockSpec(memory_space=pltpu.HBM)
 ANY = pl.BlockSpec(memory_space=pl.ANY)
@@ -104,7 +104,7 @@
     return pl.pallas_call(
         edges_kernel,
         in_specs=[HBM],
-        out_specs=[ANY, ANY],
+        out_specs=[VMEM, VMEM],
         out_shape=[shape, shape],
         scratch_shapes=[pltpu.SemaphoreType.DMA((2,))],
         name="edges",
@@ -560,8 +560,8 @@
     first_message = exchanged(message, False)
     first_two = two_away(moment2, 0)
     second_two = two_away(moment2, 1)
-    terms, first_edge, second_edge, first_two, second_two, late = lax.optimization_barrier(
-        (terms, first_edge, second_edge, first_two, second_two, message)
+    terms, first_edge, second_edge, late = lax.optimization_barrier(
+        (terms, first_edge, second_edge, message)
     )
     second_message = exchanged(late, True)
     pieces = upper(far_list1, far_list0, terms, *parts)

time: 65.4 us -> 64.5 us (0.986)
  waiting for transfers between devices: 6.51 us -> 5.13 us
    ppermute x2, waiting for transfers between devices: 2.59 us -> 0.01 us  [two_away(): return lax.ppermute(block, LEAF, pairs + [(b, a) for a, b in pairs])]
    ppermute x4, waiting for transfers between devices: 3.91 us -> 4.96 us  [exchanged(): return lax.ppermute(block, LEAF, pairs + [(b, a) for a, b in pairs])]
  transfers between devices with their start and end apart: 9 -> 9, of which waited for: 2 -> 2; matrix products, arithmetic and copies ran while one was open for 0% -> 0% of each run, Pallas kernels for 28% -> 29%
where the time goes in v4:
time: 64.5 us; the launch traced here: 64.1 us
  starting transfers between devices  35.5 us (55%)
  Pallas kernels  22.3 us (35%)
  waiting for transfers between devices  5.13 us (8%)
  local copies, waits for them, and re-layouts  1.05 us (2%)
    ppermute x4, starting transfers between devices, exchanged(): return lax.ppermute(block, LEAF, pairs + [(b, a) for a, b in pairs])  21 us
    pallas_call x1, Pallas kernels, near_parts(): pl.pallas_call(functools.partial(near_kernel, groups), in_specs=[SMEM] +...  7.21 us
    ppermute x2, starting transfers between devices, two_away(): return lax.ppermute(block, LEAF, pairs + [(b, a) for a, b in pairs])  6.21 us
    ppermute x4, waiting for transfers between devices, exchanged(): return lax.ppermute(block, LEAF, pairs + [(b, a) for a, b in pairs])  4.96 us
    all_to_all x1, starting transfers between devices, body(): terms = lax.all_to_all(spread, ('y', 'x'), 0, 0, tiled=True)  4.81 us
    pallas_call x1, Pallas kernels, moments(): pl.pallas_call(functools.partial(moments_kernel, groups), in_specs=[HBM]...  4.1 us
    pallas_call x1, Pallas kernels, far_parts(): pl.pallas_call(functools.partial(far_kernel, groups), in_specs=[SMEM] + [...  3.99 us
    pallas_call x1, Pallas kernels, finish(): pl.pallas_call(functools.partial(finish_kernel, groups), in_specs=[SMEM]...  3.82 us
  transfers between devices with their start and end apart: 9, of which 2 were waited for; matrix products, arithmetic and copies ran while one was open for 0% of the time, Pallas kernels for 29%

profile of v4, /device:TPU:24, one launch (start us, length us, event | category | flops | bytes accessed | tf_op | source)
XLA Modules:
  0.0 64.1 jit_solution(3544367113788193540)
XLA Ops:
  0.0 0.0 copy-start.1
  0.0 0.1 collective-permute-start.2
  0.1 1.2 %edges.1 = (bf16[2048,128]{1,0:T(8,128)(2,1)S(1)}, bf16[2048,128]{1,0:T(8,128)(2,1)S(1)}) custom-call(bf16[4096,128]{1,0:T(8,128)(2,1)} %bitcast.5), custom_call_target="tpu_custom_call" | custom-call | flops 1000000000 | bytes 1000 | tf_op jit(solution)/shard_map/edges/pallas_call | solution.py:104
  1.4 2.0 %collective-permute-start = (bf16[2048,128]{1,0:T(8,128)(2,1)S(1)}, bf16[2048,128]{1,0:T(8,128)(2,1)S(1)}, u32[]{:S(2)}, u32[]{:S(2)}) collective-permute-start(bf16[2048,128]{1,0:T(8,128)(2,1)S(1)} %get-tuple-element.17.after), channel_id=1, source_target_pairs={{0,2},{4,6},{8,10},{12,14},{16,18},{20,22},{24,26},{28,30},{32,34}... | collective-permute-start | bytes 1572872 | tf_op jit(solution)/shard_map/ppermute | solution.py:58
  3.4 9.2 %collective-permute-start.1 = (bf16[2048,128]{1,0:T(8,128)(2,1)S(1)}, bf16[2048,128]{1,0:T(8,128)(2,1)}, u32[]{:S(2)}, u32[]{:S(2)}) collective-permute-start(bf16[2048,128]{1,0:T(8,128)(2,1)S(1)} %get-tuple-element.19), channel_id=1, source_target_pairs={{2,4},{6,8},{10,12},{14,16},{18,20},{22,24},{26,28},{30,32},{34,36... | collective-permute-start | bytes 1572872 | tf_op jit(solution)/shard_map/ppermute | solution.py:58
  12.6 4.1 %moments.1 = (bf16[2176,128]{1,0:T(8,128)(2,1)}, bf16[128,128]{1,0:T(8,128)(2,1)}, bf16[16,128,128]{2,1,0:T(8,128)(2,1)}, bf16[16,128,128]{2,1,0:T(8,128)(2,1)S(...) custom-call(bf16[4096,128]{1,0:T(8,128)(2,1)} %bitcast.6, bf16[16,256,128]{2,1,0:T(8,128)(2,1)} %basis.3, ...), custom_call_target="tpu_custom_call" | custom-call | flops 1000000000 | bytes 1000 | tf_op jit(solution)/shard_map/moments/pallas_call | solution.py:199
  16.7 4.8 %all-to-all-start = ((bf16[16,128,128]{2,1,0:T(8,128)(2,1)}), bf16[16,128,128]{2,1,0:T(8,128)(2,1)S(1)}, u32[]{:S(2)}, u32[]{:S(2)}) async-start(bf16[16,128,128]{2,1,0:T(8,128)(2,1)} %get-tuple-element.18), calls=%async_computation | async-start | bytes 1048576 | tf_op jit(solution)/shard_map/all_to_all | solution.py:559
  21.5 0.0 collective-permute-start.5
  21.5 6.2 %collective-permute-start.6 = (bf16[128,128]{1,0:T(8,128)(2,1)}, bf16[128,128]{1,0:T(8,128)(2,1)S(1)}, u32[]{:S(2)}, u32[]{:S(2)}) collective-permute-start(bf16[128,128]{1,0:T(8,128)(2,1)} %get-tuple-element.28), channel_id=1, source_target_pairs={{4,8},{6,10},{12,16},{14,18},{20,24},{22,26},{28,32},{30,34},{36,4... | collective-permute-start | bytes 98312 | tf_op jit(solution)/shard_map/ppermute | solution.py:528
  27.7 0.0 copy-done.4
  27.7 0.1 copy.16.far1
  27.8 0.0 copy-done.2
  27.8 0.1 copy.17.near_list
  27.9 0.1 copy.18.far_list
  28.0 0.0 collective-permute-done.first_edge
  28.0 0.8 %copy-done.5 = bf16[2048,128]{1,0:T(8,128)(2,1)} copy-done((bf16[2048,128]{1,0:T(8,128)(2,1)}, bf16[2048,128]{1,0:T(8,128)(2,1)S(1)}, u32[]{:S(2)}) %copy-start.5) | copy-done | bytes 524312
  28.8 2.0 %collective-permute-start.3 = (bf16[2176,128]{1,0:T(8,128)(2,1)}, bf16[2176,128]{1,0:T(8,128)(2,1)S(1)}, u32[]{:S(2)}, u32[]{:S(2)}) collective-permute-start(bf16[2176,128]{1,0:T(8,128)(2,1)} %get-tuple-element.27.message), channel_id=1, source_target_pairs={{0,2},{4,6},{8,10},{12,14},{16,18},{20,22},{24,26},{28,30},{32,34}... | collective-permute-start | bytes 1671176 | tf_op jit(solution)/shard_map/ppermute | solution.py:58
  30.8 0.2 all-to-all-done.terms
  31.0 0.0 collective-permute-done.1.second_edge
  31.0 7.7 %collective-permute-start.4 = (bf16[2176,128]{1,0:T(8,128)(2,1)}, bf16[2176,128]{1,0:T(8,128)(2,1)S(1)}, u32[]{:S(2)}, u32[]{:S(2)}) collective-permute-start(bf16[2176,128]{1,0:T(8,128)(2,1)} %get-tuple-element.27.message), channel_id=1, source_target_pairs={{2,4},{6,8},{10,12},{14,16},{18,20},{22,24},{26,28},{30,32},{34,36... | collective-permute-start | bytes 1671176 | tf_op jit(solution)/shard_map/ppermute | solution.py:58
  38.7 1.9 %upper.1 = bf16[8,128,128]{2,1,0:T(8,128)(2,1)} custom-call(s32[16,4]{1,0:T(8,128)S(1)} %copy.16.far1, s32[4]{0:T(128)S(1)} %copy-done.1, bf16[16,128,128]{2,1,0:T(8,128)(2,1)S(1)} %all-to-all-done.terms, bf16[16,128,128]{2,1,0:T(8,128)(2,1)S(1)} %get-tuple-element.22.below, bf16[1,4,128,128]{3,2,1,0:T(8,128)(2,1)S(1)} %get-tuple-element.23.own_coupling1, ...), custom_call_target="tpu_custom_call" | custom-call | flops 5000000000 | bytes 1000 | tf_op jit(solution)/shard_map/upper/pallas_call | solution.py:246
  40.6 3.4 %all-to-all-start.1 = ((bf16[8,128,128]{2,1,0:T(8,128)(2,1)}), bf16[8,128,128]{2,1,0:T(8,128)(2,1)S(1)}, u32[]{:S(2)}, u32[]{:S(2)}) async-start(bf16[8,128,128]{2,1,0:T(8,128)(2,1)} %upper.1), calls=%async_computation.1 | async-start | bytes 524288 | tf_op jit(solution)/shard_map/all_to_all | solution.py:568
  44.0 0.0 collective-permute-done.2.theirs
  44.0 7.2 %near_parts.1.after.near = bf16[4096,128]{1,0:T(8,128)(2,1)S(1)} custom-call(s32[16,6]{1,0:T(8,128)S(1)} %copy.17.near_list, bf16[2048,128]{1,0:T(8,128)(2,1)} %copy-done.5, bf16[4096,128]{1,0:T(8,128)(2,1)} %bitcast.7, bf16[2048,128]{1,0:T(8,128)(2,1)} %collective-permute-done.1.second_edge, bf16[16,3,256,256]{3,2,1,0:T(8,128)(2,1)} %mine.1, ...), custom_call_target="tpu_custom_call" | custom-call | flops 5000000000 | bytes 1000 | tf_op jit(solution)/shard_map/near_parts/pallas_call | solution.py:323
  51.3 0.0 copy-start
  51.3 0.0 collective-permute-done.3.first_message
  51.3 5.0 %collective-permute-done.4.second_message = bf16[2176,128]{1,0:T(8,128)(2,1)S(1)} collective-permute-done((bf16[2176,128]{1,0:T(8,128)(2,1)}, bf16[2176,128]{1,0:T(8,128)(2,1)S(1)}, u32[]{:S(2)}, u32[]{:S(2)}) %collective-permute-start.4) | collective-permute-done | bytes 557088 | tf_op jit(solution)/shard_map/ppermute | solution.py:58
  56.2 4.0 %far_parts.1.far = bf16[2048,128]{1,0:T(8,128)(2,1)S(1)} custom-call(s32[16,8]{1,0:T(8,128)S(1)} %copy.18.far_list, bf16[4096,128]{1,0:T(8,128)(2,1)S(1)} %near_parts.1.after.near, bf16[2176,128]{1,0:T(8,128)(2,1)S(1)} %collective-permute-done.3.first_message, bf16[2176,128]{1,0:T(8,128)(2,1)} %get-tuple-element.27.message, ...), custom_call_target="tpu_custom_call" | custom-call | flops 20000000000 | bytes 1000 | tf_op jit(solution)/shard_map/far_parts/pallas_call | solution.py:398
  60.2 0.0 collective-permute-done.5.first_two
  60.2 0.0 collective-permute-done.6.second_two
  60.3 0.0 all-to-all-done.1.pieces
  60.3 3.8 %finish.1 = bf16[4096,128]{1,0:T(8,128)(2,1)} custom-call(s32[1,4]{1,0:T(1,128)S(1)} %copy-done, bf16[8,128,128]{2,1,0:T(8,128)(2,1)S(1)} %all-to-all-done.1.pieces, bf16[4096,128]{1,0:T(8,128)(2,1)S(1)} %near_parts.1.after.near, bf16[2048,128]{1,0:T(8,128)(2,1)S(1)} %far_parts.1.far, bf16[2176,128]{1,0:T(8,128)(2,1)S(1)} %collective-permute-done.3.first_message, ...), custom_call_target="tpu_custom_call" | custom-call | flops 1000000000 | bytes 1000 | tf_op jit(solution)/shard_map/finish/pallas_call | solution.py:504
  (7 shorter events, 0.0 us)
Async XLA Ops:
  0.0 27.7 %copy-start.4 = (s32[16,4]{0,1:T(4,128)S(1)}, s32[16,4]{0,1:T(4,128)}, u32[]{:S(2)}) copy-start(s32[16,4]{0,1:T(4,128)} %param.28) | copy-start | bytes 772
  0.0 27.8 %copy-start.2 = (s32[16,6]{0,1:T(8,128)S(1)}, s32[16,6]{0,1:T(8,128)}, u32[]{:S(2)}) copy-start(s32[16,6]{0,1:T(8,128)} %param.25) | copy-start | bytes 1156
  0.0 27.9 %copy-start.3 = (s32[16,8]{0,1:T(8,128)S(1)}, s32[16,8]{0,1:T(8,128)}, u32[]{:S(2)}) copy-start(s32[16,8]{0,1:T(8,128)} %param.26) | copy-start | bytes 1540
  0.0 38.7 %copy-start.1 = (s32[4]{0:T(128)S(1)}, s32[4]{0:T(128)}, u32[]{:S(2)}) copy-start(s32[4]{0:T(128)} %far0.1) | copy-start | bytes 52
  0.0 44.0 %collective-permute-start.2 = (bf16[16,3,256,256]{3,2,1,0:T(8,128)(2,1)}, bf16[16,3,256,256]{3,2,1,0:T(8,128)(2,1)}, u32[]{:S(2)}, u32[]{:S(2)}) collective-permute-start(bf16[16,3,256,256]{3,2,1,0:T(8,128)(2,1)} %mine.1), channel_id=1, source_target_pairs={{0,1},{1,0},{2,3},{3,2},{4,5},{5,4},{6,7},{7,6},{8,9},{9,8},{10,11... | collective-permute-start | bytes 18874376 | tf_op jit(solution)/shard_map/ppermute | solution.py:48
  1.4 26.6 %collective-permute-start = (bf16[2048,128]{1,0:T(8,128)(2,1)S(1)}, bf16[2048,128]{1,0:T(8,128)(2,1)S(1)}, u32[]{:S(2)}, u32[]{:S(2)}) collective-permute-start(bf16[2048,128]{1,0:T(8,128)(2,1)S(1)} %get-tuple-element.17.after), channel_id=1, source_target_pairs={{0,2},{4,6},{8,10},{12,14},{16,18},{20,22},{24,26},{28,30},{32,34}... | collective-permute-start | bytes 1572872 | tf_op jit(solution)/shard_map/ppermute | solution.py:58
  3.4 27.6 %collective-permute-start.1 = (bf16[2048,128]{1,0:T(8,128)(2,1)S(1)}, bf16[2048,128]{1,0:T(8,128)(2,1)}, u32[]{:S(2)}, u32[]{:S(2)}) collective-permute-start(bf16[2048,128]{1,0:T(8,128)(2,1)S(1)} %get-tuple-element.19), channel_id=1, source_target_pairs={{2,4},{6,8},{10,12},{14,16},{18,20},{22,24},{26,28},{30,32},{34,36... | collective-permute-start | bytes 1572872 | tf_op jit(solution)/shard_map/ppermute | solution.py:58
  16.7 14.3 %all-to-all-start = ((bf16[16,128,128]{2,1,0:T(8,128)(2,1)}), bf16[16,128,128]{2,1,0:T(8,128)(2,1)S(1)}, u32[]{:S(2)}, u32[]{:S(2)}) async-start(bf16[16,128,128]{2,1,0:T(8,128)(2,1)} %get-tuple-element.18), calls=%async_computation | async-start | bytes 1048576 | tf_op jit(solution)/shard_map/all_to_all | solution.py:559
  21.5 38.7 %collective-permute-start.5 = (bf16[128,128]{1,0:T(8,128)(2,1)}, bf16[128,128]{1,0:T(8,128)(2,1)S(1)}, u32[]{:S(2)}, u32[]{:S(2)}) collective-permute-start(bf16[128,128]{1,0:T(8,128)(2,1)} %get-tuple-element.28), channel_id=1, source_target_pairs={{0,4},{2,6},{8,12},{10,14},{16,20},{18,22},{24,28},{26,30},{32,36}... | collective-permute-start | bytes 98312 | tf_op jit(solution)/shard_map/ppermute | solution.py:528
  21.5 38.7 %collective-permute-start.6 = (bf16[128,128]{1,0:T(8,128)(2,1)}, bf16[128,128]{1,0:T(8,128)(2,1)S(1)}, u32[]{:S(2)}, u32[]{:S(2)}) collective-permute-start(bf16[128,128]{1,0:T(8,128)(2,1)} %get-tuple-element.28), channel_id=1, source_target_pairs={{4,8},{6,10},{12,16},{14,18},{20,24},{22,26},{28,32},{30,34},{36,4... | collective-permute-start | bytes 98312 | tf_op jit(solution)/shard_map/ppermute | solution.py:528
  28.0 0.8 %copy-start.5 = (bf16[2048,128]{1,0:T(8,128)(2,1)}, bf16[2048,128]{1,0:T(8,128)(2,1)S(1)}, u32[]{:S(2)}) copy-start(bf16[2048,128]{1,0:T(8,128)(2,1)S(1)} %collective-permute-done.first_edge) | copy-start | bytes 1572868
  28.8 22.5 %collective-permute-start.3 = (bf16[2176,128]{1,0:T(8,128)(2,1)}, bf16[2176,128]{1,0:T(8,128)(2,1)S(1)}, u32[]{:S(2)}, u32[]{:S(2)}) collective-permute-start(bf16[2176,128]{1,0:T(8,128)(2,1)} %get-tuple-element.27.message), channel_id=1, source_target_pairs={{0,2},{4,6},{8,10},{12,14},{16,18},{20,22},{24,26},{28,30},{32,34}... | collective-permute-start | bytes 1671176 | tf_op jit(solution)/shard_map/ppermute | solution.py:58
  31.0 25.3 %collective-permute-start.4 = (bf16[2176,128]{1,0:T(8,128)(2,1)}, bf16[2176,128]{1,0:T(8,128)(2,1)S(1)}, u32[]{:S(2)}, u32[]{:S(2)}) collective-permute-start(bf16[2176,128]{1,0:T(8,128)(2,1)} %get-tuple-element.27.message), channel_id=1, source_target_pairs={{2,4},{6,8},{10,12},{14,16},{18,20},{22,24},{26,28},{30,32},{34,36... | collective-permute-start | bytes 1671176 | tf_op jit(solution)/shard_map/ppermute | solution.py:58
  40.6 19.6 %all-to-all-start.1 = ((bf16[8,128,128]{2,1,0:T(8,128)(2,1)}), bf16[8,128,128]{2,1,0:T(8,128)(2,1)S(1)}, u32[]{:S(2)}, u32[]{:S(2)}) async-start(bf16[8,128,128]{2,1,0:T(8,128)(2,1)} %upper.1), calls=%async_computation.1 | async-start | bytes 524288 | tf_op jit(solution)/shard_map/all_to_all | solution.py:568
  51.3 9.0 %copy-start = (s32[1,4]{1,0:T(1,128)S(1)}, s32[1,4]{1,0:T(1,128)}, u32[]{:S(2)}) copy-start(s32[1,4]{1,0:T(1,128)} %far2.1) | copy-start | bytes 52
